TPU v7x, 512 devices: a whole 4x8x8 slice. The times are simulated.
512 devices in a mesh: ta: 32 (over y, x), gz: 8 (over z_hi, core), gy: 2 (over z_lo).
Axes of the slice: x: 4, y: 8, z: 8 (z_hi: 4, z_lo: 2; z = z_hi * 2 + z_lo), core: 2. Of those that a mesh axis runs over, the one named last changes fastest.
Arguments:
- solution_x: bfloat16 [4, 24, 32, 32, 256], P(None, None, 'ta', 'gz', 'gy'), may hold values from -6 to 6
- solution_y: bfloat16 [4, 24, 32, 32, 256], P(None, None, 'ta', 'gz', 'gy'), may hold values from -6 to 6
- links: bfloat16 [4, 18, 32, 32, 256], P(None, None, 'ta', 'gz', 'gy'), may hold values from -3.5 to 3.5
- pole_coef: float32 [4], replicated, may hold values from 0.02 to 0.2
Outputs:
- momentum: float32 [4, 18, 32, 32, 256], P(None, None, 'ta', 'gz', 'gy')
All inputs are finite; a program needn't handle non-finite values.
Results may differ from a plain program's by a relative error of at most 0.0044.
Values may be sent and summed in bfloat16 or wider, within the bound.
No kernel may reach another device: no remote copies, remote signals or barrier semaphores. Data moves between devices by JAX's collectives and lax.ppermute only.
A program may use at most 64 MiB of HBM per device.

v0:
```python
import jax
import jax.numpy as jnp
import numpy as np
from jax import lax
from jax.experimental import pallas as pl
from jax.experimental.pallas import tpu as pltpu
from jax.sharding import PartitionSpec as P

F32, BF16 = jnp.float32, jnp.bfloat16
LANES, CX = 128, 64
PLANES = [(0, 1), (0, 2), (0, 3), (1, 2), (1, 3), (2, 3)]
T_PAIR = ((0, 3), (1, 3))
Z_PAIRS = [((0, 2), (1, 2)), ((0, 1), (2, 3))]
OFF = [(0, 1), (0, 2), (1, 2)]

T_LINK, T_L, T_CORNER, T_ROWS = 384, 600, 720, 736
Y_REST, Y_HALF, Y_CORNER, Y_ROWS = 192, 168, 360, 384
TY_ROWS = 48
Z_LINK, Z_L, Z_ROWS = 96, 150, 192

G_UN1, G_UM1 = 8, 160
G_LM, G_LN, G_LMN, G_L0 = 312, 392, 472, 552
G_UM, G_UN = 624, 768
G_ROWS = 920


def spin_tables():
    one = np.array([[0, 1], [1, 0]], dtype=complex)
    two = np.array([[0, -1j], [1j, 0]], dtype=complex)
    three = np.array([[1, 0], [0, -1]], dtype=complex)
    pauli = [one, two, three]
    blocks = [-1j * one, -1j * two, -1j * three, np.eye(2, dtype=complex)]
    insert = []
    for m, n in PLANES:
        b, c = blocks[m], blocks[n]
        up = 0.5j * (b @ c.conj().T - c @ b.conj().T)
        low = 0.5j * (b.conj().T @ c - c.conj().T @ b)
        entry = []
        for block in (up, low):
            for j in range(3):
                sign = np.trace(block @ pauli[j]).real / 2
                if abs(sign) > 0.5:
                    entry.append((j, float(sign)))
        insert.append(entry)
    return blocks, insert


BLOCKS, INSERT = spin_tables()


def lane_index():
    return lax.broadcasted_iota(jnp.int32, (8, LANES), 1)


def roll64(v):
    return pltpu.roll(v, CX, 1)


def x_next(v):
    lanes = lax.broadcasted_iota(jnp.int32, v.shape, 1)
    return jnp.where(lanes % CX == CX - 1, pltpu.roll(v, CX - 1, 1), pltpu.roll(v, LANES - 1, 1))


def low_half(v):
    return lax.broadcasted_iota(jnp.int32, v.shape, 1) < CX


def pair_spinors(src, base, dst):
    for k in range(4):
        dst[pl.ds(192 * (k % 2) + k // 2, 96, stride=2), :] = src[base + 96 * k : base + 96 * k + 96, :].astype(F32)


def spin_part(ref, p, ri, spin, col):
    row = 192 * p + 8 * (ri * 12 + spin * 3 + col)
    return ref[row : row + 8, :]


def half_component(ref, p, ri, spin, col, m, sign):
    base = spin_part(ref, p, ri, spin, col)
    for b in range(2):
        coeff = sign * BLOCKS[m][spin, b]
        if coeff.real != 0:
            low = spin_part(ref, p, ri, 2 + b, col)
            base = base + low if coeff.real > 0 else base - low
        if coeff.imag != 0:
            low = spin_part(ref, p, 1 - ri, 2 + b, col)
            positive = (coeff.imag > 0) == (ri == 1)
            base = base + low if positive else base - low
    return base


def far_halves(xs, ys, m):
    for p in range(2):
        for term, (ref, sign) in enumerate(((xs, -1.0), (ys, 1.0))):
            for ri in range(2):
                for spin in range(2):
                    for col in range(3):
                        index = p * 24 + term * 12 + ri * 6 + spin * 3 + col
                        yield index, half_component(ref, p, ri, spin, col, m, sign)


def insertions(xs, ys, weights, ls, ld):
    matrices = []
    for chi in range(2):
        cross = {}
        third = {}

        def add(store, key, value):
            store[key] = value if key not in store else store[key] + value

        for p in range(2):
            w = weights[8 * p : 8 * p + 8, :]
            x = [[[spin_part(xs, p, ri, 2 * chi + s, c) for ri in range(2)] for c in range(3)] for s in range(2)]
            y = [[[spin_part(ys, p, ri, 2 * chi + s, c) * w for ri in range(2)] for c in range(3)] for s in range(2)]
            for c in range(3):
                for d in range(3):
                    for left, right in ((x, y), (y, x)):
                        a, b = left[1][c], right[0][d]
                        add(cross, (c, d, 0), a[0] * b[0] + a[1] * b[1])
                        add(cross, (c, d, 1), a[1] * b[0] - a[0] * b[1])
            for c in range(3):
                value = (x[0][c][0] * y[0][c][0] + x[0][c][1] * y[0][c][1]) - (
                    x[1][c][0] * y[1][c][0] + x[1][c][1] * y[1][c][1]
                )
                add(third, (c,), value)
            for c, d in OFF:
                for left, right in ((x, y), (y, x)):
                    for s in range(2):
                        a, b = left[s][c], right[s][d]
                        re = a[0] * b[0] + a[1] * b[1]
                        im = a[1] * b[0] - a[0] * b[1]
                        add(third, (c, d, 0), re if s == 0 else -re)
                        add(third, (c, d, 1), im if s == 0 else -im)
        first = [2.0 * cross[c, c, 0] for c in range(3)]
        second = [2.0 * cross[c, c, 1] for c in range(3)]
        last = [2.0 * third[(c,)] for c in range(3)]
        for c, d in OFF:
            first += [cross[c, d, 0] + cross[d, c, 0], cross[c, d, 1] - cross[d, c, 1]]
            second += [cross[c, d, 1] + cross[d, c, 1], cross[d, c, 0] - cross[c, d, 0]]
            last += [third[c, d, 0], third[c, d, 1]]
        matrices.append((first, second, last))
    for plane in range(6):
        (up, up_sign), (low, low_sign) = INSERT[plane]
        for e in range(9):
            a, b = matrices[0][up][e], matrices[1][low][e]
            value = a + b if up_sign * low_sign > 0 else a - b
            row = (plane * 9 + e) * 8
            ls[row : row + 8, :] = value if up_sign > 0 else -value
    ld[...] = ls[pl.ds(0, 216, stride=2), :] + ls[pl.ds(1, 216, stride=2), :]


def plane_rows(m, n):
    base = 36 * PLANES.index((min(m, n), max(m, n)))
    return slice(base, base + 36)


def first_kernel(
    all_ref, coef, xs, ys, us, ld, weights, t_out, y_out, ty_out, z_out, ls, ts, hs, ds, ys2, zs
):
    pair_spinors(all_ref, 0, xs)
    pair_spinors(all_ref, 384, ys)
    us[...] = all_ref[768:1056, :].astype(F32)
    even = lax.broadcasted_iota(jnp.int32, (8, LANES), 0) % 2 == 0
    spread = [jnp.broadcast_to(coef[0:1, k : k + 1], (8, LANES)) for k in range(4)]
    for p in range(2):
        weights[8 * p : 8 * p + 8, :] = jnp.where(even, spread[p], spread[p + 2])
    insertions(xs, ys, weights, ls, ld)
    for index, value in far_halves(xs, ys, 3):
        ts[8 * index : 8 * index + 8, :] = value
    ts[T_LINK : T_LINK + 216, :] = us[0:216, :]
    for slot, m in enumerate((0, 1, 2)):
        ts[T_L + 36 * slot : T_L + 36 * slot + 36, :] = ld[plane_rows(m, 3), :]
    ts[T_L + 108 : T_ROWS, :] = jnp.zeros((T_ROWS - T_L - 108, LANES), F32)
    ts[T_CORNER : T_CORNER + 9, :] = ld[pl.ds(plane_rows(2, 3).start, 9, stride=4), :]
    t_out[...] = ts[...].astype(BF16)
    for index, value in far_halves(xs, ys, 1):
        hs[8 * index : 8 * index + 8, :] = value
    first, second = hs[0:192, :], hs[192:384, :]
    ys2[0:192, :] = jnp.where(low_half(first), first, roll64(second))
    for slot, n in enumerate((0, 2, 3)):
        ds[72 * slot : 72 * slot + 72, :] = us[72 * n : 72 * n + 72, :]
        ds[216 + 36 * slot : 216 + 36 * slot + 36, :] = ld[plane_rows(1, n), :]
    ds[324:336, :] = jnp.zeros((12, LANES), F32)
    first, second = ds[0:Y_HALF, :], ds[Y_HALF : 2 * Y_HALF, :]
    ys2[Y_REST : Y_REST + Y_HALF, :] = jnp.where(low_half(first), first, roll64(second))
    ys2[Y_CORNER:Y_ROWS, :] = jnp.zeros((Y_ROWS - Y_CORNER, LANES), F32)
    ys2[Y_CORNER : Y_CORNER + 9, :] = roll64(ld[pl.ds(plane_rows(1, 2).start, 9, stride=4), :])
    y_out[...] = ys2[...].astype(BF16)
    ds[0:36, :] = roll64(ld[plane_rows(1, 3), :])
    ty_out[...] = ds[0:TY_ROWS, :].astype(BF16)
    for index, value in far_halves(xs, ys, 2):
        hs[8 * index : 8 * index + 8, :] = value
    zs[0:48, :] = hs[pl.ds(0, 48, stride=8), :]
    zs[48:96, :] = hs[pl.ds(1, 48, stride=8), :]
    for slot, n in enumerate((0, 1, 3)):
        zs[Z_LINK + 18 * slot : Z_LINK + 18 * slot + 18, :] = us[pl.ds(72 * n, 18, stride=4), :]
        zs[Z_L + 9 * slot : Z_L + 9 * slot + 9, :] = ld[pl.ds(plane_rows(2, n).start, 9, stride=4), :]
    zs[Z_L + 27 : Z_ROWS, :] = jnp.zeros((Z_ROWS - Z_L - 27, LANES), F32)
    z_out[...] = zs[...].astype(BF16)


def full(ref, base):
    def get(ri, c, d):
        return ref[pl.ds(base + 8 * (ri * 9 + c * 3 + d), 8), :]

    return get


def herm(ref, base):
    def get(ri, c, d):
        if c == d:
            return None if ri else ref[pl.ds(base + 8 * c, 8), :]
        low, high = min(c, d), max(c, d)
        value = ref[pl.ds(base + 8 * (3 + 2 * OFF.index((low, high)) + ri), 8), :]
        return -value if ri and c > d else value

    return get


def dagger(get):
    def other(ri, c, d):
        value = get(ri, d, c)
        return -value if ri and value is not None else value

    return other


def dot(left, right, ri, c, d):
    total = None
    for e in range(3):
        for part in range(2):
            a, b = left(part, c, e), right(ri ^ part, e, d)
            if a is None or b is None:
                continue
            term = a * b
            if ri == 0 and part == 1:
                total = -term if total is None else total - term
            else:
                total = term if total is None else total + term
    return total


def held(get):
    table = {(ri, c, d): get(ri, c, d) for ri in range(2) for c in range(3) for d in range(3)}
    return lambda ri, c, d: table[ri, c, d]


def product(left, right, extra=None):
    table = {}
    for c in range(3):
        for d in range(3):
            for ri in range(2):
                value = dot(left, right, ri, c, d)
                if extra is not None:
                    value = value + extra(ri, c, d)
                table[ri, c, d] = value
    return lambda ri, c, d: table[ri, c, d]


def keep(ref, base, get):
    for ri in range(2):
        for c in range(3):
            for d in range(3):
                ref[pl.ds(base + 8 * (ri * 9 + c * 3 + d), 8), :] = get(ri, c, d)
    return full(ref, base)


def anti(left, right):
    entries = [dot(left, right, 1, c, c) for c in range(3)]
    for c, d in OFF:
        entries.append(dot(left, right, 0, c, d) - dot(left, right, 0, d, c))
        entries.append(dot(left, right, 1, c, d) + dot(left, right, 1, d, c))
    return entries


def stage_near(xs, ys, weights, near, base, m):
    for p in range(2):
        for term, (ref, sign) in enumerate(((ys, -1.0), (xs, 1.0))):
            for ri in range(2):
                for spin in range(2):
                    for col in range(3):
                        index = p * 24 + term * 12 + ri * 6 + spin * 3 + col
                        row = base + 8 * index
                        near[row : row + 8, :] = half_component(ref, p, ri, spin, col, m, sign) * weights[8 * p : 8 * p + 8, :]


def hop_sums(far, near, far_base, near_base, hop, hop_base):
    sums = {}
    for p in range(2):
        for term in range(2):
            for spin in range(2):

                def part(ref, base, ri, col):
                    return ref[pl.ds(base + 8 * (p * 24 + term * 12 + ri * 6 + spin * 3 + col), 8), :]

                a = [[part(far, far_base, ri, c) for ri in range(2)] for c in range(3)]
                b = [[part(near, near_base, ri, c) for ri in range(2)] for c in range(3)]
                for c in range(3):
                    for d in range(3):
                        re = a[c][0] * b[d][0] + a[c][1] * b[d][1]
                        im = a[c][1] * b[d][0] - a[c][0] * b[d][1]
                        if (c, d) in sums:
                            sums[c, d] = (sums[c, d][0] + re, sums[c, d][1] + im)
                        else:
                            sums[c, d] = (re, im)
    for c in range(3):
        for d in range(3):
            for ri in range(2):
                hop[pl.ds(hop_base + 8 * (ri * 9 + c * 3 + d), 8), :] = sums[c, d][ri]


class Neighbours:
    def __init__(self, geo, us, ld, tf=None, yf=None, tyf=None, zf=None):
        self.geo, self.us, self.ld, self.tf, self.yf, self.tyf, self.zf = geo, us, ld, tf, yf, tyf, zf

    def link(self, n):
        return self.us[72 * n : 72 * n + 72, :]

    def came_y(self, row, count):
        pieces = []
        if row < Y_HALF:
            stop = min(row + count, Y_HALF)
            pieces.append(roll64(self.yf[Y_REST + row : Y_REST + stop, :]))
            count, row = count - (stop - row), stop
        if count:
            pieces.append(self.yf[Y_REST + row - Y_HALF : Y_REST + row - Y_HALF + count, :])
        return pieces[0] if len(pieces) == 1 else jnp.concatenate(pieces, axis=0)

    def y_next(self, here, came):
        return jnp.where(low_half(here), roll64(here), came)

    def put(self, base, h, value):
        self.geo[pl.ds(base + h, value.shape[0], stride=2), :] = value

    def put_z(self, base, h, value, face):
        self.geo[pl.ds(base + h - 2, value.shape[0], stride=2), :] = value
        self.geo[pl.ds(base + h + 6, face.shape[0], stride=8), :] = face

    def link_next(self, base, h, n, m):
        slot = [k for k in range(4) if k != m].index(n)
        if m == 0:
            self.put(base, h, x_next(self.link(n)))
        elif m == 1:
            self.put(base, h, self.y_next(self.link(n), self.came_y(72 * slot, 72)))
        elif m == 2:
            self.put_z(base, h, self.link(n), self.zf[Z_LINK + 18 * slot : Z_LINK + 18 * slot + 18, :])
        else:
            self.put(base, h, self.tf[72 * slot : 72 * slot + 72, :])

    def here(self, m, n):
        return self.ld[plane_rows(m, n), :]

    def from_t(self, n):
        return self.tf[216 + 36 * n : 216 + 36 * n + 36, :]

    def from_y(self, n):
        slot = (0, 2, 3).index(n)
        return self.y_next(self.here(1, n), self.came_y(216 + 36 * slot, 36))

    def z_face(self, n):
        slot = (0, 1, 3).index(n)
        return self.zf[Z_L + 9 * slot : Z_L + 9 * slot + 9, :]

    def insertion_next(self, base, h, n, m):
        if m == 0:
            self.put(base, h, x_next(self.here(m, n)))
        elif m == 1:
            self.put(base, h, self.from_y(n))
        elif m == 2:
            self.put_z(base, h, self.here(m, n), self.z_face(n))
        else:
            self.put(base, h, self.from_t(n))

    def corner(self, base, h, m, n):
        if m == 0 and n == 1:
            self.put(base, h, x_next(self.from_y(0)))
        elif m == 0 and n == 2:
            self.put_z(base, h, x_next(self.here(0, 2)), x_next(self.z_face(0)))
        elif m == 0:
            self.put(base, h, x_next(self.from_t(0)))
        elif m == 1 and n == 2:
            face = self.z_face(1)
            came = self.zf[Z_ROWS + 16 : Z_ROWS + 25, :]
            self.put_z(base, h, self.from_y(2), jnp.where(low_half(face), roll64(face), came))
        elif m == 1:
            self.put(base, h, self.y_next(self.from_t(1), self.tyf[0:36, :]))
        else:
            self.put_z(base, h, self.from_t(2), self.zf[Z_ROWS : Z_ROWS + 9, :])

    def stage(self, base, pair):
        for h in range(2):
            m, n = pair[h]
            self.put(base + G_UM, h, self.link(m))
            self.put(base + G_UN, h, self.link(n))
            self.link_next(base + G_UN1, h, n, m)
            self.link_next(base + G_UM1, h, m, n)
            self.insertion_next(base + G_LM, h, n, m)
            self.insertion_next(base + G_LN, h, m, n)
            self.corner(base + G_LMN, h, m, n)
            self.put(base + G_L0, h, self.here(m, n))


def plane_force(geo, g, work, acc, a):
    um, un = full(geo, g + G_UM), full(geo, g + G_UN)
    un1, um1 = full(geo, g + G_UN1), full(geo, g + G_UM1)
    lm, ln, lmn, l0 = (herm(geo, g + k) for k in (G_LM, G_LN, G_LMN, G_L0))
    loop = keep(work, 0, product(un1, dagger(um1)))
    inner = keep(work, 144, product(un1, lmn))
    first = product(lm, loop)
    inner = keep(work, 288, product(inner, dagger(um1), first))
    inner = keep(work, 144, product(loop, ln, inner))
    inner = keep(work, 288, product(um, inner))
    loop = keep(work, 144, product(um, loop))
    whole = keep(work, 0, product(loop, dagger(un)))
    common = anti(inner, dagger(un))
    to_m = anti(whole, l0)
    to_n = anti(l0, whole)
    for e in range(9):
        scale = 0.5 if e < 3 else 0.25
        acc[pl.ds(a + 8 * e, 8), :] = scale * (common[e] + to_m[e])
        acc[pl.ds(a + 72 + 8 * e, 8), :] = scale * (common[e] + to_n[e])


def xy_kernel(xs, ys, weights, y_ref, hop, yf, far, near):
    yf[...] = y_ref[0:Y_REST, :].astype(F32)
    for index, value in far_halves(xs, ys, 0):
        far[8 * index : 8 * index + 8, :] = x_next(value)
    stage_near(xs, ys, weights, near, 0, 0)
    low = lane_index() < CX
    for index, value in far_halves(xs, ys, 1):
        row = 384 + 8 * index
        came = yf[8 * (index % 24) : 8 * (index % 24) + 8, :]
        if index < 24:
            far[row : row + 8, :] = roll64(jnp.where(low, came, value))
        else:
            far[row : row + 8, :] = jnp.where(low, roll64(value), came)
    stage_near(xs, ys, weights, near, 384, 1)

    def one_hop(m, carry):
        base = pl.multiple_of(m * 384, 8)
        hop_sums(far, near, base, base, hop, pl.multiple_of(m * 144, 8))
        return carry

    lax.fori_loop(0, 2, one_hop, 0)


def t_kernel(xs, ys, us, ld, weights, t_ref, y_ref, ty_ref, hop, acc, tf, yf, tyf, near, geo, work):
    tf[...] = t_ref[384:T_ROWS, :].astype(F32)
    yf[...] = y_ref[...].astype(F32)
    tyf[...] = ty_ref[...].astype(F32)
    geo[920:1304, :] = t_ref[0:384, :].astype(F32)
    stage_near(xs, ys, weights, near, 0, 3)
    hop_sums(geo, near, 920, 0, hop, 0)
    Neighbours(geo, us, ld, tf, yf, tyf).stage(0, T_PAIR)
    plane_force(geo, 0, work, acc, 0)


def last_kernel(
    xs, ys, us, ld, weights, t_ref, y_ref, z_ref, hop_xy, hop_t, acc_t, out,
    tf, yf, zf, far, near, hop, geo, work, acc,
):
    tf[...] = t_ref[384:T_ROWS, :].astype(F32)
    yf[...] = y_ref[...].astype(F32)
    zf[...] = z_ref[0 : Z_ROWS + 32, :].astype(F32)
    for index, value in far_halves(xs, ys, 2):
        far[8 + 8 * index - 2 : 8 + 8 * index + 6, :] = value
    far[pl.ds(8 + 6, 48, stride=8), :] = zf[0:48, :]
    far[pl.ds(8 + 7, 48, stride=8), :] = zf[48:96, :]
    stage_near(xs, ys, weights, near, 0, 2)
    hop_sums(far, near, 8, 0, hop, 0)
    places = Neighbours(geo, us, ld, tf, yf, None, zf)
    for pair in range(2):
        places.stage(G_ROWS * pair, Z_PAIRS[pair])

    def one_pair(pair, carry):
        plane_force(geo, pl.multiple_of(pair * G_ROWS, 8), work, acc, pl.multiple_of(pair * 144, 8))
        return carry

    lax.fori_loop(0, 2, one_pair, 0)
    acc[288:432, :] = acc_t[...]

    even = lax.broadcasted_iota(jnp.int32, (8, LANES), 0) % 2 == 0
    places.put(0, 0, places.link(0))
    places.put(0, 1, places.link(1))
    places.put(144, 0, places.link(2))
    places.put(144, 1, places.link(3))
    halves = [((hop_xy, 0), (hop_xy, 144)), ((hop, 0), (hop_t, 0))]
    for pair in range(2):
        table = {}
        for ri in range(2):
            for c in range(3):
                for d in range(3):
                    row = 8 * (ri * 9 + c * 3 + d)
                    a, b = (ref[base + row : base + row + 8, :] for ref, base in halves[pair])
                    table[ri, c, d] = jnp.where(even, a + pltpu.roll(a, 7, 0), b + pltpu.roll(b, 1, 0))
        entries = anti(full(geo, 144 * pair), lambda ri, c, d: table[ri, c, d])
        for e in range(9):
            row = 432 + 72 * pair + 8 * e
            acc[row : row + 8, :] = entries[e] if e < 3 else 0.5 * entries[e]

    sources = [
        [(0, 0), (2, 0), (4, 0), (6, 0)],
        [(0, 1), (3, 0), (4, 1), (6, 1)],
        [(1, 0), (1, 1), (2, 1), (7, 0)],
        [(3, 1), (5, 0), (5, 1), (7, 1)],
    ]
    zero = jnp.zeros((4, LANES), F32)
    for m in range(4):
        values = []
        for e in range(9):
            total = None
            for slot, h in sources[m]:
                piece = acc[pl.ds(72 * slot + 8 * e + h, 4, stride=2), :]
                total = piece if total is None else total + piece
            values.append(total)
        trace = (values[0] + values[1] + values[2]) * (1.0 / 3.0)
        for c in range(3):
            for d in range(3):
                if c == d:
                    re, im = zero, values[c] - trace
                else:
                    e = 3 + 2 * OFF.index((min(c, d), max(c, d)))
                    re, im = (values[e] if c < d else -values[e]), values[e + 1]
                row = 72 * m + 4 * (3 * c + d)
                out[row : row + 4, :] = re
                out[row + 36 : row + 40, :] = im


def vmem(rows):
    return pltpu.VMEM((rows, LANES), F32)


IN_VMEM = pl.BlockSpec(memory_space=pltpu.VMEM)


def call(kernel, name, in_specs, outs, scratch, flops, out_specs=IN_VMEM):
    shapes = [jax.ShapeDtypeStruct((rows, LANES), kind) for rows, kind in outs]
    return pl.pallas_call(
        kernel,
        out_shape=shapes,
        in_specs=in_specs,
        out_specs=[out_specs] * len(shapes),
        scratch_shapes=[vmem(k) if isinstance(k, int) else k for k in scratch],
        compiler_params=pltpu.CompilerParams(vmem_limit_bytes=24 * 1024 * 1024),
        cost_estimate=pl.CostEstimate(flops=flops, bytes_accessed=1000000, transcendentals=0),
        name=name,
    )


def passed_back(block, *axes):
    sizes = [lax.axis_size(axis) for axis in axes]
    route = []
    for place in np.ndindex(*sizes):
        source = [(k + 1) % size for k, size in zip(place, sizes)]
        route.append((int(np.ravel_multi_index(source, sizes)), int(np.ravel_multi_index(place, sizes))))
    return lax.ppermute(block, axes if len(axes) > 1 else axes[0], route)


def shards(solution_x, solution_y, links, pole_coef):
    fields = jnp.concatenate(
        [solution_x.reshape(384, LANES), solution_y.reshape(384, LANES), links.reshape(288, LANES)]
    )
    xs, ys, us, local, weights, to_t, to_y, to_ty, to_z = call(
        first_kernel,
        "pack_faces",
        [IN_VMEM] * 2,
        [(384, F32), (384, F32), (288, F32), (216, F32), (16, F32), (T_ROWS, BF16), (Y_ROWS, BF16), (TY_ROWS, BF16), (Z_ROWS, BF16)],
        [432, T_ROWS, 384, 336, Y_ROWS, Z_ROWS],
        2000000,
    )(fields, pole_coef.reshape(1, 4))
    t_came = passed_back(to_t, "ta")
    y_came = passed_back(to_y, "gy")
    ty_came = passed_back(to_ty, "ta", "gy")
    z_block = jnp.concatenate(
        [to_z, t_came[T_CORNER : T_CORNER + 16], y_came[Y_CORNER : Y_CORNER + 16], ty_came[TY_ROWS - 16 :]]
    )
    z_came = passed_back(z_block, "gz")
    (hop_xy,) = call(
        xy_kernel, "hop_xy", [IN_VMEM] * 4, [(288, F32)], [Y_REST, 768, 768], 2000000
    )(xs, ys, weights, y_came)
    hop_t, acc_t = call(
        t_kernel,
        "force_t",
        [IN_VMEM] * 8,
        [(144, F32), (144, F32)],
        [T_ROWS - 384, Y_ROWS, TY_ROWS, 384, 1304, 432],
        2000000,
    )(xs, ys, us, local, weights, t_came, y_came, ty_came)
    (force,) = call(
        last_kernel,
        "force",
        [IN_VMEM] * 11,
        [(288, F32)],
        [T_ROWS - 384, Y_ROWS, Z_ROWS + 32, 400, 384, 144, 2 * G_ROWS, 432, 576],
        4000000,
        out_specs=pl.BlockSpec(),
    )(xs, ys, us, local, weights, t_came, y_came, z_came, hop_xy, hop_t, acc_t)
    return force.reshape(links.shape)


def solution(mesh):
    placed = P(None, None, "ta", "gz", "gy")
    return jax.shard_map(
        shards, mesh=mesh, in_specs=(placed, placed, placed, P()), out_specs=placed, check_vma=False
    )
```

profile of v0, /device:TPU:129, one launch (start us, length us, event | category | flops | bytes accessed | tf_op | source)
XLA Modules:
  0.0 31.3 jit_solution(7417265403966516684)
XLA Ops:
  0.0 1.0 %pad_maximum_fusion.all_ref = bf16[1056,128]{1,0:T(8,128)(2,1)S(1)} fusion(bf16[288,128]{1,0:T(8,128)(2,1)} %bitcast.10, bf16[384,128]{1,0:T(8,128)(2,1)} %bitcast.8, bf16[384,128]{1,0:T(8,128)(2,1)} %bitcast.9), kind=kLoop, calls=%fused_computation | loop fusion | flops 811008 | bytes 540672 | tf_op jit(solution)/shard_map/concatenate | solution.py:560
  1.0 0.0 copy-start
  1.0 0.6 %copy-done = f32[4]{0:T(128)S(1)} copy-done((f32[4]{0:T(128)S(1)}, f32[4]{0:T(128)}, u32[]{:S(2)}) %copy-start) | copy-done | bytes 40
  1.7 0.4 %pack_faces.1 = (f32[384,128]{1,0:T(8,128)S(1)}, f32[384,128]{1,0:T(8,128)S(1)}, f32[288,128]{1,0:T(8,128)S(1)}, f32[216,128]{1,0:T(8,128)S(1)}, f32[16,128]{1,0...) custom-call(bf16[1056,128]{1,0:T(8,128)(2,1)S(1)} %pad_maximum_fusio, ...), custom_call_target="tpu_custom_call" | custom-call | flops 2000000 | bytes 1000000 | tf_op jit(solution)/shard_map/pack_faces/pallas_call | solution.py:563
  2.1 7.3 %collective-permute-start = (bf16[736,128]{1,0:T(8,128)(2,1)S(1)}, bf16[736,128]{1,0:T(8,128)(2,1)S(1)}, u32[]{:S(2)}, u32[]{:S(2)}) collective-permute-start(bf16[736,128]{1,0:T(8,128)(2,1)S(1)} %get-tuple-element.21), channel_id=1, source_target_pairs={{16,0},{32,16},{48,32},{64,48},{80,64},{96,80},{112,96},{128,112},... | collective-permute-start | bytes 565256 | tf_op jit(solution)/shard_map/ppermute | solution.py:556
  9.4 4.0 %collective-permute-start.1 = (bf16[384,128]{1,0:T(8,128)(2,1)S(1)}, bf16[384,128]{1,0:T(8,128)(2,1)S(1)}, u32[]{:S(2)}, u32[]{:S(2)}) collective-permute-start(bf16[384,128]{1,0:T(8,128)(2,1)S(1)} %get-tuple-element.22), channel_id=1, source_target_pairs={{1,0},{0,1},{3,2},{2,3},{5,4},{4,5},{7,6},{6,7},{9,8},{8,9},{11,10... | collective-permute-start | bytes 294920 | tf_op jit(solution)/shard_map/ppermute | solution.py:556
  13.4 2.2 %collective-permute-start.2 = (bf16[48,128]{1,0:T(8,128)(2,1)S(1)}, bf16[48,128]{1,0:T(8,128)(2,1)S(1)}, u32[]{:S(2)}, u32[]{:S(2)}) collective-permute-start(bf16[48,128]{1,0:T(8,128)(2,1)S(1)} %get-tuple-element.24), channel_id=1, source_target_pairs={{17,0},{16,1},{33,16},{32,17},{49,32},{48,33},{65,48},{64,49},{81,... | collective-permute-start | bytes 36872 | tf_op jit(solution)/shard_map/ppermute | solution.py:556
  15.6 3.1 %collective-permute-done.2.ty_ref = bf16[48,128]{1,0:T(8,128)(2,1)S(1)} collective-permute-done((bf16[48,128]{1,0:T(8,128)(2,1)S(1)}, bf16[48,128]{1,0:T(8,128)(2,1)S(1)}, u32[]{:S(2)}, u32[]{:S(2)}) %collective-permute-start.2) | collective-permute-done | bytes 12320 | tf_op jit(solution)/shard_map/ppermute | solution.py:556
  18.7 0.0 collective-permute-done.1.y_ref
  18.7 0.0 collective-permute-done.t_ref
  18.7 4.3 %collective-permute-start.3 = (bf16[240,128]{1,0:T(8,128)(2,1)S(1)}, bf16[240,128]{1,0:T(8,128)(2,1)S(1)}, u32[]{:S(2)}, u32[]{:S(2)}) collective-permute-start(bf16[240,128]{1,0:T(8,128)(2,1)S(1)} %pad_maximum_fusion.1), channel_id=1, source_target_pairs={{2,0},{4,2},{6,4},{8,6},{10,8},{12,10},{14,12},{0,14},{3,1},{5,3},... | collective-permute-start | bytes 184328 | tf_op jit(solution)/shard_map/ppermute | solution.py:556
  23.0 0.4 %hop_xy.1 = f32[288,128]{1,0:T(8,128)S(1)} custom-call(f32[384,128]{1,0:T(8,128)S(1)} %get-tuple-element.16.xs, f32[384,128]{1,0:T(8,128)S(1)} %get-tuple-element.17.ys, f32[16,128]{1,0:T(8,128)S(1)} %get-tuple-element.20.weights, bf16[384,128]{1,0:T(8,128)(2,1)S(1)} %collective-permute-done.1.y_ref), custom_call_target="tpu_custom_call" | custom-call | flops 2000000 | bytes 1000000 | tf_op jit(solution)/shard_map/hop_xy/pallas_call | solution.py:578
  23.5 0.5 %force_t.1 = (f32[144,128]{1,0:T(8,128)S(1)}, f32[144,128]{1,0:T(8,128)S(1)}) custom-call(f32[384,128]{1,0:T(8,128)S(1)} %get-tuple-element.16.xs, f32[384,128]{1,0:T(8,128)S(1)} %get-tuple-element.17.ys, f32[288,128]{1,0:T(8,128)S(1)} %get-tuple-element.18.us, f32[216,128]{1,0:T(8,128)S(1)} %get-tuple-element.19.ld, ...), custom_call_target="tpu_custom_call" | custom-call | flops 2000000 | bytes 1000000 | tf_op jit(solution)/shard_map/force_t/pallas_call | solution.py:581
  24.0 5.7 %collective-permute-done.3.z_ref = bf16[240,128]{1,0:T(8,128)(2,1)S(1)} collective-permute-done((bf16[240,128]{1,0:T(8,128)(2,1)S(1)}, bf16[240,128]{1,0:T(8,128)(2,1)S(1)}, u32[]{:S(2)}, u32[]{:S(2)}) %collective-permute-start.3) | collective-permute-done | bytes 61472 | tf_op jit(solution)/shard_map/ppermute | solution.py:556
  29.7 1.6 %force.1 = f32[288,128]{1,0:T(8,128)} custom-call(f32[384,128]{1,0:T(8,128)S(1)} %get-tuple-element.16.xs, f32[384,128]{1,0:T(8,128)S(1)} %get-tuple-element.17.ys, f32[288,128]{1,0:T(8,128)S(1)} %get-tuple-element.18.us, f32[216,128]{1,0:T(8,128)S(1)} %get-tuple-element.19.ld, f32[16,128]{1,0:T(8,128)S(1)} %get-tuple-element.20.weights, ...), custom_call_target="tpu_custom_call" | custom-call | flops 4000000 | bytes 1000000 | tf_op jit(solution)/shard_map/force/pallas_call | solution.py:589
  (4 shorter events, 0.0 us)
Async XLA Ops:
  1.0 0.7 %copy-start = (f32[4]{0:T(128)S(1)}, f32[4]{0:T(128)}, u32[]{:S(2)}) copy-start(f32[4]{0:T(128)} %param.7) | copy-start | bytes 52
  2.1 16.7 %collective-permute-start = (bf16[736,128]{1,0:T(8,128)(2,1)S(1)}, bf16[736,128]{1,0:T(8,128)(2,1)S(1)}, u32[]{:S(2)}, u32[]{:S(2)}) collective-permute-start(bf16[736,128]{1,0:T(8,128)(2,1)S(1)} %get-tuple-element.21), channel_id=1, source_target_pairs={{16,0},{32,16},{48,32},{64,48},{80,64},{96,80},{112,96},{128,112},... | collective-permute-start | bytes 565256 | tf_op jit(solution)/shard_map/ppermute | solution.py:556
  9.4 9.4 %collective-permute-start.1 = (bf16[384,128]{1,0:T(8,128)(2,1)S(1)}, bf16[384,128]{1,0:T(8,128)(2,1)S(1)}, u32[]{:S(2)}, u32[]{:S(2)}) collective-permute-start(bf16[384,128]{1,0:T(8,128)(2,1)S(1)} %get-tuple-element.22), channel_id=1, source_target_pairs={{1,0},{0,1},{3,2},{2,3},{5,4},{4,5},{7,6},{6,7},{9,8},{8,9},{11,10... | collective-permute-start | bytes 294920 | tf_op jit(solution)/shard_map/ppermute | solution.py:556
  13.4 5.3 %collective-permute-start.2 = (bf16[48,128]{1,0:T(8,128)(2,1)S(1)}, bf16[48,128]{1,0:T(8,128)(2,1)S(1)}, u32[]{:S(2)}, u32[]{:S(2)}) collective-permute-start(bf16[48,128]{1,0:T(8,128)(2,1)S(1)} %get-tuple-element.24), channel_id=1, source_target_pairs={{17,0},{16,1},{33,16},{32,17},{49,32},{48,33},{65,48},{64,49},{81,... | collective-permute-start | bytes 36872 | tf_op jit(solution)/shard_map/ppermute | solution.py:556
  18.7 10.9 %collective-permute-start.3 = (bf16[240,128]{1,0:T(8,128)(2,1)S(1)}, bf16[240,128]{1,0:T(8,128)(2,1)S(1)}, u32[]{:S(2)}, u32[]{:S(2)}) collective-permute-start(bf16[240,128]{1,0:T(8,128)(2,1)S(1)} %pad_maximum_fusion.1), channel_id=1, source_target_pairs={{2,0},{4,2},{6,4},{8,6},{10,8},{12,10},{14,12},{0,14},{3,1},{5,3},... | collective-permute-start | bytes 184328 | tf_op jit(solution)/shard_map/ppermute | solution.py:556
where the time goes:
time: 31.6 us; the launch traced here: 31.3 us
  starting transfers between devices  17.8 us (56%)
  waiting for transfers between devices  8.87 us (28%)
  Pallas kernels  2.93 us (9%)
  other arithmetic  1 us (3%)
  local copies, waits for them, and re-layouts  0.66 us (2%)
    ppermute x4, starting transfers between devices, passed_back(): return lax.ppermute(block, axes if len(axes) > 1 else axes[0], route)  17.8 us
    ppermute x4, waiting for transfers between devices, passed_back(): return lax.ppermute(block, axes if len(axes) > 1 else axes[0], route)  8.87 us
    pallas_call x1, Pallas kernels, shards(): call(last_kernel, 'force', [IN_VMEM] * 11, [(288, F32)], [T_ROWS - 384, Y...  1.63 us
    concatenate x1, other arithmetic, shards(): jnp.concatenate([solution_x.reshape(384, LANES), solution_y.reshape(384,...  0.99 us
    unnamed x2, local copies, waits for them, and re-layouts  0.65 us
  transfers between devices with their start and end apart: 4, of which 2 were waited for; matrix products, arithmetic and copies ran while one was open for 0% of the time, Pallas kernels for 3%

commit v1 on v0

--- a/solution.py
+++ b/solution.py
@@ -155,16 +155,24 @@
 
 
 def first_kernel(
-    all_ref, coef, xs, ys, us, ld, weights, t_out, y_out, ty_out, z_out, ls, ts, hs, ds, ys2, zs
+    x_hbm, y_hbm, u_hbm, coef_hbm, xs, ys, us, ld, weights, t_out, y_out, ty_out, z_out,
+    x_ref, y_ref, u_ref, coef, ls, ts, hs, ds, ys2, zs, sems,
 ):
-    pair_spinors(all_ref, 0, xs)
-    pair_spinors(all_ref, 384, ys)
-    us[...] = all_ref[768:1056, :].astype(F32)
+    pairs = ((coef_hbm, coef), (x_hbm, x_ref), (y_hbm, y_ref), (u_hbm, u_ref))
+    copies = [pltpu.make_async_copy(source, target, sems.at[k]) for k, (source, target) in enumerate(pairs)]
+    for copy in copies:
+        copy.start()
+    copies[1].wait()
+    pair_spinors(x_ref, 0, xs)
+    copies[2].wait()
+    pair_spinors(y_ref, 0, ys)
+    copies[0].wait()
     even = lax.broadcasted_iota(jnp.int32, (8, LANES), 0) % 2 == 0
-    spread = [jnp.broadcast_to(coef[0:1, k : k + 1], (8, LANES)) for k in range(4)]
     for p in range(2):
-        weights[8 * p : 8 * p + 8, :] = jnp.where(even, spread[p], spread[p + 2])
+        weights[8 * p : 8 * p + 8, :] = jnp.where(even, coef[p], coef[p + 2])
     insertions(xs, ys, weights, ls, ld)
+    copies[3].wait()
+    us[...] = u_ref[...].astype(F32)
     for index, value in far_halves(xs, ys, 3):
         ts[8 * index : 8 * index + 8, :] = value
     ts[T_LINK : T_LINK + 216, :] = us[0:216, :]
@@ -557,17 +565,16 @@
 
 
 def shards(solution_x, solution_y, links, pole_coef):
-    fields = jnp.concatenate(
-        [solution_x.reshape(384, LANES), solution_y.reshape(384, LANES), links.reshape(288, LANES)]
-    )
+    inputs = [solution_x.reshape(384, LANES), solution_y.reshape(384, LANES), links.reshape(288, LANES), pole_coef]
     xs, ys, us, local, weights, to_t, to_y, to_ty, to_z = call(
         first_kernel,
         "pack_faces",
-        [IN_VMEM] * 2,
+        [pl.BlockSpec(memory_space=pltpu.HBM)] * 4,
         [(384, F32), (384, F32), (288, F32), (216, F32), (16, F32), (T_ROWS, BF16), (Y_ROWS, BF16), (TY_ROWS, BF16), (Z_ROWS, BF16)],
-        [432, T_ROWS, 384, 336, Y_ROWS, Z_ROWS],
+        [pltpu.VMEM((384, LANES), BF16)] * 2
+        + [pltpu.VMEM((288, LANES), BF16), pltpu.SMEM((4,), F32), 432, T_ROWS, 384, 336, Y_ROWS, Z_ROWS, pltpu.SemaphoreType.DMA((4,))],
         2000000,
-    )(fields, pole_coef.reshape(1, 4))
+    )(*[pltpu.with_memory_space_constraint(array, pltpu.HBM) for array in inputs])
     t_came = passed_back(to_t, "ta")
     y_came = passed_back(to_y, "gy")
     ty_came = passed_back(to_ty, "ta", "gy")

time: 31.6 us -> 30.8 us (0.975)
  other arithmetic: 1 us -> 0.01 us
  Pallas kernels: 2.93 us -> 3.87 us
  local copies, waits for them, and re-layouts: 0.66 us -> 0.01 us
    concatenate x1 -> x0, other arithmetic: 0.99 us -> none  [shards(): jnp.concatenate([solution_x.reshape(384, LANES), solution_y.reshape(384,...]
    pallas_call x1, Pallas kernels: 0.4 us -> 1.35 us  [shards(): call(first_kernel, 'pack_faces', [pl.BlockSpec(memory_space=pltpu.HBM)] *...]
    unnamed x2 -> x0, local copies, waits for them, and re-layouts: 0.65 us -> none
where the time goes in v1:
time: 30.8 us; the launch traced here: 30.6 us
  starting transfers between devices  17.8 us (58%)
  waiting for transfers between devices  8.87 us (29%)
  Pallas kernels  3.87 us (13%)
    ppermute x4, starting transfers between devices, passed_back(): return lax.ppermute(block, axes if len(axes) > 1 else axes[0], route)  17.8 us
    ppermute x4, waiting for transfers between devices, passed_back(): return lax.ppermute(block, axes if len(axes) > 1 else axes[0], route)  8.87 us
    pallas_call x1, Pallas kernels, shards(): call(last_kernel, 'force', [IN_VMEM] * 11, [(288, F32)], [T_ROWS - 384, Y...  1.63 us
    pallas_call x1, Pallas kernels, shards(): call(first_kernel, 'pack_faces', [pl.BlockSpec(memory_space=pltpu.HBM)] *...  1.35 us
  transfers between devices with their start and end apart: 4, of which 2 were waited for; matrix products, arithmetic and copies ran while one was open for 0% of the time, Pallas kernels for 3%

profile of v1, /device:TPU:129, one launch (start us, length us, event | category | flops | bytes accessed | tf_op | source)
XLA Modules:
  0.0 30.6 jit_solution(12474986901636086185)
XLA Ops:
  0.0 1.3 %pack_faces.1 = (f32[384,128]{1,0:T(8,128)S(1)}, f32[384,128]{1,0:T(8,128)S(1)}, f32[288,128]{1,0:T(8,128)S(1)}, f32[216,128]{1,0:T(8,128)S(1)}, f32[16,128]{1,0...) custom-call(bf16[384,128]{1,0:T(8,128)(2,1)} %bitcast.6, ...), custom_call_target="tpu_custom_call" | custom-call | flops 2000000 | bytes 1000000 | tf_op jit(solution)/shard_map/pack_faces/pallas_call | solution.py:569
  1.4 7.3 %collective-permute-start = (bf16[736,128]{1,0:T(8,128)(2,1)S(1)}, bf16[736,128]{1,0:T(8,128)(2,1)S(1)}, u32[]{:S(2)}, u32[]{:S(2)}) collective-permute-start(bf16[736,128]{1,0:T(8,128)(2,1)S(1)} %get-tuple-element.21), channel_id=1, source_target_pairs={{16,0},{32,16},{48,32},{64,48},{80,64},{96,80},{112,96},{128,112},... | collective-permute-start | bytes 565256 | tf_op jit(solution)/shard_map/ppermute | solution.py:564
  8.7 4.0 %collective-permute-start.1 = (bf16[384,128]{1,0:T(8,128)(2,1)S(1)}, bf16[384,128]{1,0:T(8,128)(2,1)S(1)}, u32[]{:S(2)}, u32[]{:S(2)}) collective-permute-start(bf16[384,128]{1,0:T(8,128)(2,1)S(1)} %get-tuple-element.22), channel_id=1, source_target_pairs={{1,0},{0,1},{3,2},{2,3},{5,4},{4,5},{7,6},{6,7},{9,8},{8,9},{11,10... | collective-permute-start | bytes 294920 | tf_op jit(solution)/shard_map/ppermute | solution.py:564
  12.7 2.2 %collective-permute-start.2 = (bf16[48,128]{1,0:T(8,128)(2,1)S(1)}, bf16[48,128]{1,0:T(8,128)(2,1)S(1)}, u32[]{:S(2)}, u32[]{:S(2)}) collective-permute-start(bf16[48,128]{1,0:T(8,128)(2,1)S(1)} %get-tuple-element.24), channel_id=1, source_target_pairs={{17,0},{16,1},{33,16},{32,17},{49,32},{48,33},{65,48},{64,49},{81,... | collective-permute-start | bytes 36872 | tf_op jit(solution)/shard_map/ppermute | solution.py:564
  14.9 3.1 %collective-permute-done.2.ty_ref = bf16[48,128]{1,0:T(8,128)(2,1)S(1)} collective-permute-done((bf16[48,128]{1,0:T(8,128)(2,1)S(1)}, bf16[48,128]{1,0:T(8,128)(2,1)S(1)}, u32[]{:S(2)}, u32[]{:S(2)}) %collective-permute-start.2) | collective-permute-done | bytes 12320 | tf_op jit(solution)/shard_map/ppermute | solution.py:564
  18.0 0.0 collective-permute-done.1.y_ref
  18.0 0.0 collective-permute-done.t_ref
  18.0 4.3 %collective-permute-start.3 = (bf16[240,128]{1,0:T(8,128)(2,1)S(1)}, bf16[240,128]{1,0:T(8,128)(2,1)S(1)}, u32[]{:S(2)}, u32[]{:S(2)}) collective-permute-start(bf16[240,128]{1,0:T(8,128)(2,1)S(1)} %pad_maximum_fusion), channel_id=1, source_target_pairs={{2,0},{4,2},{6,4},{8,6},{10,8},{12,10},{14,12},{0,14},{3,1},{5,3},... | collective-permute-start | bytes 184328 | tf_op jit(solution)/shard_map/ppermute | solution.py:564
  22.3 0.4 %hop_xy.1 = f32[288,128]{1,0:T(8,128)S(1)} custom-call(f32[384,128]{1,0:T(8,128)S(1)} %get-tuple-element.16.xs, f32[384,128]{1,0:T(8,128)S(1)} %get-tuple-element.17.ys, f32[16,128]{1,0:T(8,128)S(1)} %get-tuple-element.20.weights, bf16[384,128]{1,0:T(8,128)(2,1)S(1)} %collective-permute-done.1.y_ref), custom_call_target="tpu_custom_call" | custom-call | flops 2000000 | bytes 1000000 | tf_op jit(solution)/shard_map/hop_xy/pallas_call | solution.py:585
  22.7 0.5 %force_t.1 = (f32[144,128]{1,0:T(8,128)S(1)}, f32[144,128]{1,0:T(8,128)S(1)}) custom-call(f32[384,128]{1,0:T(8,128)S(1)} %get-tuple-element.16.xs, f32[384,128]{1,0:T(8,128)S(1)} %get-tuple-element.17.ys, f32[288,128]{1,0:T(8,128)S(1)} %get-tuple-element.18.us, f32[216,128]{1,0:T(8,128)S(1)} %get-tuple-element.19.ld, ...), custom_call_target="tpu_custom_call" | custom-call | flops 2000000 | bytes 1000000 | tf_op jit(solution)/shard_map/force_t/pallas_call | solution.py:588
  23.3 5.7 %collective-permute-done.3.z_ref = bf16[240,128]{1,0:T(8,128)(2,1)S(1)} collective-permute-done((bf16[240,128]{1,0:T(8,128)(2,1)S(1)}, bf16[240,128]{1,0:T(8,128)(2,1)S(1)}, u32[]{:S(2)}, u32[]{:S(2)}) %collective-permute-start.3) | collective-permute-done | bytes 61472 | tf_op jit(solution)/shard_map/ppermute | solution.py:564
  29.0 1.6 %force.1 = f32[288,128]{1,0:T(8,128)} custom-call(f32[384,128]{1,0:T(8,128)S(1)} %get-tuple-element.16.xs, f32[384,128]{1,0:T(8,128)S(1)} %get-tuple-element.17.ys, f32[288,128]{1,0:T(8,128)S(1)} %get-tuple-element.18.us, f32[216,128]{1,0:T(8,128)S(1)} %get-tuple-element.19.ld, f32[16,128]{1,0:T(8,128)S(1)} %get-tuple-element.20.weights, ...), custom_call_target="tpu_custom_call" | custom-call | flops 4000000 | bytes 1000000 | tf_op jit(solution)/shard_map/force/pallas_call | solution.py:596
  (4 shorter events, 0.0 us)
Async XLA Ops:
  1.4 16.7 %collective-permute-start = (bf16[736,128]{1,0:T(8,128)(2,1)S(1)}, bf16[736,128]{1,0:T(8,128)(2,1)S(1)}, u32[]{:S(2)}, u32[]{:S(2)}) collective-permute-start(bf16[736,128]{1,0:T(8,128)(2,1)S(1)} %get-tuple-element.21), channel_id=1, source_target_pairs={{16,0},{32,16},{48,32},{64,48},{80,64},{96,80},{112,96},{128,112},... | collective-permute-start | bytes 565256 | tf_op jit(solution)/shard_map/ppermute | solution.py:564
  8.7 9.4 %collective-permute-start.1 = (bf16[384,128]{1,0:T(8,128)(2,1)S(1)}, bf16[384,128]{1,0:T(8,128)(2,1)S(1)}, u32[]{:S(2)}, u32[]{:S(2)}) collective-permute-start(bf16[384,128]{1,0:T(8,128)(2,1)S(1)} %get-tuple-element.22), channel_id=1, source_target_pairs={{1,0},{0,1},{3,2},{2,3},{5,4},{4,5},{7,6},{6,7},{9,8},{8,9},{11,10... | collective-permute-start | bytes 294920 | tf_op jit(solution)/shard_map/ppermute | solution.py:564
  12.7 5.3 %collective-permute-start.2 = (bf16[48,128]{1,0:T(8,128)(2,1)S(1)}, bf16[48,128]{1,0:T(8,128)(2,1)S(1)}, u32[]{:S(2)}, u32[]{:S(2)}) collective-permute-start(bf16[48,128]{1,0:T(8,128)(2,1)S(1)} %get-tuple-element.24), channel_id=1, source_target_pairs={{17,0},{16,1},{33,16},{32,17},{49,32},{48,33},{65,48},{64,49},{81,... | collective-permute-start | bytes 36872 | tf_op jit(solution)/shard_map/ppermute | solution.py:564
  18.0 10.9 %collective-permute-start.3 = (bf16[240,128]{1,0:T(8,128)(2,1)S(1)}, bf16[240,128]{1,0:T(8,128)(2,1)S(1)}, u32[]{:S(2)}, u32[]{:S(2)}) collective-permute-start(bf16[240,128]{1,0:T(8,128)(2,1)S(1)} %pad_maximum_fusion), channel_id=1, source_target_pairs={{2,0},{4,2},{6,4},{8,6},{10,8},{12,10},{14,12},{0,14},{3,1},{5,3},... | collective-permute-start | bytes 184328 | tf_op jit(solution)/shard_map/ppermute | solution.py:564

commit v2 on v1

--- a/solution.py
+++ b/solution.py
@@ -13,9 +13,9 @@
 Z_PAIRS = [((0, 2), (1, 2)), ((0, 1), (2, 3))]
 OFF = [(0, 1), (0, 2), (1, 2)]
 
-T_LINK, T_L, T_CORNER, T_ROWS = 384, 600, 720, 736
+L_XT, L_ZT, L_CORNER, L_ROWS = 48, 84, 128, 144
+T_LINK, T_ROWS = 384, 608
 Y_REST, Y_HALF, Y_CORNER, Y_ROWS = 192, 168, 360, 384
-TY_ROWS = 48
 Z_LINK, Z_L, Z_ROWS = 96, 150, 192
 
 G_UN1, G_UM1 = 8, 160
@@ -155,8 +155,8 @@
 
 
 def first_kernel(
-    x_hbm, y_hbm, u_hbm, coef_hbm, xs, ys, us, ld, weights, t_out, y_out, ty_out, z_out,
-    x_ref, y_ref, u_ref, coef, ls, ts, hs, ds, ys2, zs, sems,
+    x_hbm, y_hbm, u_hbm, coef_hbm, xs, ys, us, ld, weights, tl_out,
+    x_ref, y_ref, u_ref, coef, ls, ds, sems,
 ):
     pairs = ((coef_hbm, coef), (x_hbm, x_ref), (y_hbm, y_ref), (u_hbm, u_ref))
     copies = [pltpu.make_async_copy(source, target, sems.at[k]) for k, (source, target) in enumerate(pairs)]
@@ -173,14 +173,15 @@
     insertions(xs, ys, weights, ls, ld)
     copies[3].wait()
     us[...] = u_ref[...].astype(F32)
-    for index, value in far_halves(xs, ys, 3):
-        ts[8 * index : 8 * index + 8, :] = value
-    ts[T_LINK : T_LINK + 216, :] = us[0:216, :]
-    for slot, m in enumerate((0, 1, 2)):
-        ts[T_L + 36 * slot : T_L + 36 * slot + 36, :] = ld[plane_rows(m, 3), :]
-    ts[T_L + 108 : T_ROWS, :] = jnp.zeros((T_ROWS - T_L - 108, LANES), F32)
-    ts[T_CORNER : T_CORNER + 9, :] = ld[pl.ds(plane_rows(2, 3).start, 9, stride=4), :]
-    t_out[...] = ts[...].astype(BF16)
+    ds[...] = jnp.zeros((L_ROWS, LANES), F32)
+    ds[0:36, :] = ld[plane_rows(1, 3), :]
+    ds[L_XT : L_XT + 36, :] = ld[plane_rows(0, 3), :]
+    ds[L_ZT : L_ZT + 36, :] = ld[plane_rows(2, 3), :]
+    ds[L_CORNER : L_CORNER + 9, :] = ld[pl.ds(plane_rows(2, 3).start, 9, stride=4), :]
+    tl_out[...] = ds[...].astype(BF16)
+
+
+def y_pack_kernel(xs, ys, us, ld, y_out, hs, ds, ys2):
     for index, value in far_halves(xs, ys, 1):
         hs[8 * index : 8 * index + 8, :] = value
     first, second = hs[0:192, :], hs[192:384, :]
@@ -194,8 +195,17 @@
     ys2[Y_CORNER:Y_ROWS, :] = jnp.zeros((Y_ROWS - Y_CORNER, LANES), F32)
     ys2[Y_CORNER : Y_CORNER + 9, :] = roll64(ld[pl.ds(plane_rows(1, 2).start, 9, stride=4), :])
     y_out[...] = ys2[...].astype(BF16)
-    ds[0:36, :] = roll64(ld[plane_rows(1, 3), :])
-    ty_out[...] = ds[0:TY_ROWS, :].astype(BF16)
+
+
+def t_pack_kernel(xs, ys, us, t_out, ts):
+    for index, value in far_halves(xs, ys, 3):
+        ts[8 * index : 8 * index + 8, :] = value
+    ts[T_LINK : T_LINK + 216, :] = us[0:216, :]
+    ts[T_LINK + 216 : T_ROWS, :] = jnp.zeros((T_ROWS - T_LINK - 216, LANES), F32)
+    t_out[...] = ts[...].astype(BF16)
+
+
+def z_pack_kernel(xs, ys, us, ld, tl_ref, z_out, hs, zs):
     for index, value in far_halves(xs, ys, 2):
         hs[8 * index : 8 * index + 8, :] = value
     zs[0:48, :] = hs[pl.ds(0, 48, stride=8), :]
@@ -204,6 +214,7 @@
         zs[Z_LINK + 18 * slot : Z_LINK + 18 * slot + 18, :] = us[pl.ds(72 * n, 18, stride=4), :]
         zs[Z_L + 9 * slot : Z_L + 9 * slot + 9, :] = ld[pl.ds(plane_rows(2, n).start, 9, stride=4), :]
     zs[Z_L + 27 : Z_ROWS, :] = jnp.zeros((Z_ROWS - Z_L - 27, LANES), F32)
+    zs[Z_ROWS : Z_ROWS + 16, :] = tl_ref[L_CORNER:L_ROWS, :].astype(F32)
     z_out[...] = zs[...].astype(BF16)
 
 
@@ -318,8 +329,8 @@
 
 
 class Neighbours:
-    def __init__(self, geo, us, ld, tf=None, yf=None, tyf=None, zf=None):
-        self.geo, self.us, self.ld, self.tf, self.yf, self.tyf, self.zf = geo, us, ld, tf, yf, tyf, zf
+    def __init__(self, geo, us, ld, tf=None, tl=None, yf=None, zf=None):
+        self.geo, self.us, self.ld, self.tf, self.tl, self.yf, self.zf = geo, us, ld, tf, tl, yf, zf
 
     def link(self, n):
         return self.us[72 * n : 72 * n + 72, :]
@@ -359,7 +370,8 @@
         return self.ld[plane_rows(m, n), :]
 
     def from_t(self, n):
-        return self.tf[216 + 36 * n : 216 + 36 * n + 36, :]
+        row = (L_XT, 0, L_ZT)[n]
+        return self.tl[row : row + 36, :]
 
     def from_y(self, n):
         slot = (0, 2, 3).index(n)
@@ -391,7 +403,7 @@
             came = self.zf[Z_ROWS + 16 : Z_ROWS + 25, :]
             self.put_z(base, h, self.from_y(2), jnp.where(low_half(face), roll64(face), came))
         elif m == 1:
-            self.put(base, h, self.y_next(self.from_t(1), self.tyf[0:36, :]))
+            self.put(base, h, self.y_next(self.from_t(1), roll64(self.yf[Y_ROWS : Y_ROWS + 36, :])))
         else:
             self.put_z(base, h, self.from_t(2), self.zf[Z_ROWS : Z_ROWS + 9, :])
 
@@ -452,22 +464,23 @@
     lax.fori_loop(0, 2, one_hop, 0)
 
 
-def t_kernel(xs, ys, us, ld, weights, t_ref, y_ref, ty_ref, hop, acc, tf, yf, tyf, near, geo, work):
-    tf[...] = t_ref[384:T_ROWS, :].astype(F32)
+def t_kernel(xs, ys, us, ld, weights, tl_ref, t_ref, y_ref, hop, acc, tl, tf, yf, near, geo, work):
+    tl[...] = tl_ref[...].astype(F32)
+    tf[...] = t_ref[T_LINK:T_ROWS, :].astype(F32)
     yf[...] = y_ref[...].astype(F32)
-    tyf[...] = ty_ref[...].astype(F32)
     geo[920:1304, :] = t_ref[0:384, :].astype(F32)
     stage_near(xs, ys, weights, near, 0, 3)
     hop_sums(geo, near, 920, 0, hop, 0)
-    Neighbours(geo, us, ld, tf, yf, tyf).stage(0, T_PAIR)
+    Neighbours(geo, us, ld, tf, tl, yf).stage(0, T_PAIR)
     plane_force(geo, 0, work, acc, 0)
 
 
 def last_kernel(
-    xs, ys, us, ld, weights, t_ref, y_ref, z_ref, hop_xy, hop_t, acc_t, out,
-    tf, yf, zf, far, near, hop, geo, work, acc,
+    xs, ys, us, ld, weights, tl_ref, t_ref, y_ref, z_ref, hop_xy, hop_t, acc_t, out,
+    tl, tf, yf, zf, far, near, hop, geo, work, acc,
 ):
-    tf[...] = t_ref[384:T_ROWS, :].astype(F32)
+    tl[...] = tl_ref[...].astype(F32)
+    tf[...] = t_ref[T_LINK:T_ROWS, :].astype(F32)
     yf[...] = y_ref[...].astype(F32)
     zf[...] = z_ref[0 : Z_ROWS + 32, :].astype(F32)
     for index, value in far_halves(xs, ys, 2):
@@ -476,7 +489,7 @@
     far[pl.ds(8 + 7, 48, stride=8), :] = zf[48:96, :]
     stage_near(xs, ys, weights, near, 0, 2)
     hop_sums(far, near, 8, 0, hop, 0)
-    places = Neighbours(geo, us, ld, tf, yf, None, zf)
+    places = Neighbours(geo, us, ld, tf, tl, yf, zf)
     for pair in range(2):
         places.stage(G_ROWS * pair, Z_PAIRS[pair])
 
@@ -566,20 +579,25 @@
 
 def shards(solution_x, solution_y, links, pole_coef):
     inputs = [solution_x.reshape(384, LANES), solution_y.reshape(384, LANES), links.reshape(288, LANES), pole_coef]
-    xs, ys, us, local, weights, to_t, to_y, to_ty, to_z = call(
+    xs, ys, us, local, weights, to_tl = call(
         first_kernel,
-        "pack_faces",
+        "insertions",
         [pl.BlockSpec(memory_space=pltpu.HBM)] * 4,
-        [(384, F32), (384, F32), (288, F32), (216, F32), (16, F32), (T_ROWS, BF16), (Y_ROWS, BF16), (TY_ROWS, BF16), (Z_ROWS, BF16)],
+        [(384, F32), (384, F32), (288, F32), (216, F32), (16, F32), (L_ROWS, BF16)],
         [pltpu.VMEM((384, LANES), BF16)] * 2
-        + [pltpu.VMEM((288, LANES), BF16), pltpu.SMEM((4,), F32), 432, T_ROWS, 384, 336, Y_ROWS, Z_ROWS, pltpu.SemaphoreType.DMA((4,))],
-        2000000,
+        + [pltpu.VMEM((288, LANES), BF16), pltpu.SMEM((4,), F32), 432, L_ROWS, pltpu.SemaphoreType.DMA((4,))],
+        1000000,
     )(*[pltpu.with_memory_space_constraint(array, pltpu.HBM) for array in inputs])
+    tl_came = passed_back(to_tl, "ta")
+    (to_t,) = call(t_pack_kernel, "pack_t", [IN_VMEM] * 3, [(T_ROWS, BF16)], [T_ROWS], 500000)(xs, ys, us)
     t_came = passed_back(to_t, "ta")
-    y_came = passed_back(to_y, "gy")
-    ty_came = passed_back(to_ty, "ta", "gy")
+    (to_y,) = call(y_pack_kernel, "pack_y", [IN_VMEM] * 4, [(Y_ROWS, BF16)], [384, 336, Y_ROWS], 500000)(xs, ys, us, local)
+    y_came = passed_back(jnp.concatenate([to_y, tl_came[0:48]]), "gy")
+    (to_z,) = call(z_pack_kernel, "pack_z", [IN_VMEM] * 5, [(Z_ROWS + 16, BF16)], [384, Z_ROWS + 16], 500000)(
+        xs, ys, us, local, tl_came
+    )
     z_block = jnp.concatenate(
-        [to_z, t_came[T_CORNER : T_CORNER + 16], y_came[Y_CORNER : Y_CORNER + 16], ty_came[TY_ROWS - 16 :]]
+        [to_z, y_came[Y_CORNER : Y_CORNER + 16], t_came[T_ROWS - 16 :]]
     )
     z_came = passed_back(z_block, "gz")
     (hop_xy,) = call(
@@ -590,18 +608,18 @@
         "force_t",
         [IN_VMEM] * 8,
         [(144, F32), (144, F32)],
-        [T_ROWS - 384, Y_ROWS, TY_ROWS, 384, 1304, 432],
+        [L_ROWS, T_ROWS - T_LINK, Y_ROWS + 48, 384, 1304, 432],
         2000000,
-    )(xs, ys, us, local, weights, t_came, y_came, ty_came)
+    )(xs, ys, us, local, weights, tl_came, t_came, y_came)
     (force,) = call(
         last_kernel,
         "force",
-        [IN_VMEM] * 11,
+        [IN_VMEM] * 12,
         [(288, F32)],
-        [T_ROWS - 384, Y_ROWS, Z_ROWS + 32, 400, 384, 144, 2 * G_ROWS, 432, 576],
+        [L_ROWS, T_ROWS - T_LINK, Y_ROWS + 48, Z_ROWS + 32, 400, 384, 144, 2 * G_ROWS, 432, 576],
         4000000,
         out_specs=pl.BlockSpec(),
-    )(xs, ys, us, local, weights, t_came, y_came, z_came, hop_xy, hop_t, acc_t)
+    )(xs, ys, us, local, weights, tl_came, t_came, y_came, z_came, hop_xy, hop_t, acc_t)
     return force.reshape(links.shape)
 
 

time: 30.8 us -> 30.5 us (level)
  the two profiles are of different devices: /device:TPU:129 before, /device:TPU:2 now
where the time goes in v2:
time: 30.5 us; the launch traced here: 30.3 us
  starting transfers between devices  22.6 us (74%)
  Pallas kernels  3.92 us (13%)
  waiting for transfers between devices  3.6 us (12%)
    ppermute x4, starting transfers between devices, passed_back(): return lax.ppermute(block, axes if len(axes) > 1 else axes[0], route)  22.6 us
    ppermute x4, waiting for transfers between devices, passed_back(): return lax.ppermute(block, axes if len(axes) > 1 else axes[0], route)  3.6 us
    pallas_call x1, Pallas kernels, shards(): call(last_kernel, 'force', [IN_VMEM] * 12, [(288, F32)], [L_ROWS, T_ROWS...  1.62 us
    pallas_call x1, Pallas kernels, shards(): call(first_kernel, 'insertions', [pl.BlockSpec(memory_space=pltpu.HBM)] *...  1.2 us
  transfers between devices with their start and end apart: 4, of which 2 were waited for; matrix products, arithmetic and copies ran while one was open for 0% of the time, Pallas kernels for 4%

profile of v2, /device:TPU:2, one launch (start us, length us, event | category | flops | bytes accessed | tf_op | source)
XLA Modules:
  0.0 30.3 jit_solution(15414789983380930213)
XLA Ops:
  0.0 1.2 %insertions.1 = (f32[384,128]{1,0:T(8,128)S(1)}, f32[384,128]{1,0:T(8,128)S(1)}, f32[288,128]{1,0:T(8,128)S(1)}, f32[216,128]{1,0:T(8,128)S(1)}, f32[16,128]{1,0:T(8,128)S(1)}, /*index=5*/bf16[144,128]{1,0:T(8,128)(2,1)S(1)}) custom-call(bf16[384,128]{1,0:T(8,128)(2,1)} %bitcast.6, bf16[384,128]{1,0:T(8,128)(2,1)} %bitcast.7, bf16[288,128]{1,0:T(8,128)(2,1)} %bitcast.8, ...), custom_call_target="tpu_custom_call" | custom-call | flops 1000000 | bytes 1000000 | tf_op jit(solution)/shard_map/insertions/pallas_call | solution.py:582
  1.2 7.8 %collective-permute-start = (bf16[144,128]{1,0:T(8,128)(2,1)S(1)}, bf16[144,128]{1,0:T(8,128)(2,1)S(1)}, u32[]{:S(2)}, u32[]{:S(2)}) collective-permute-start(bf16[144,128]{1,0:T(8,128)(2,1)S(1)} %get-tuple-element.18), channel_id=1, source_target_pairs={{16,0},{32,16},{48,32},{64,48},{80,64},{96,80},{112,96},{128,112},... | collective-permute-start | bytes 110600 | tf_op jit(solution)/shard_map/ppermute | solution.py:577
  9.1 2.2 %collective-permute-start.1 = (bf16[608,128]{1,0:T(8,128)(2,1)S(1)}, bf16[608,128]{1,0:T(8,128)(2,1)S(1)}, u32[]{:S(2)}, u32[]{:S(2)}) collective-permute-start(bf16[608,128]{1,0:T(8,128)(2,1)S(1)} %pack_t.1), channel_id=1, source_target_pairs={{16,0},{32,16},{48,32},{64,48},{80,64},{96,80},{112,96},{128,112},... | collective-permute-start | bytes 466952 | tf_op jit(solution)/shard_map/ppermute | solution.py:577
  11.3 0.1 pack_y.1
  11.4 0.0 collective-permute-done.tl_ref
  11.4 4.3 %collective-permute-start.2 = (bf16[432,128]{1,0:T(8,128)(2,1)S(1)}, bf16[432,128]{1,0:T(8,128)(2,1)S(1)}, u32[]{:S(2)}, u32[]{:S(2)}) collective-permute-start(bf16[432,128]{1,0:T(8,128)(2,1)S(1)} %pad_maximum_fusion), channel_id=1, source_target_pairs={{1,0},{0,1},{3,2},{2,3},{5,4},{4,5},{7,6},{6,7},{9,8},{8,9},{11,10... | collective-permute-start | bytes 331784 | tf_op jit(solution)/shard_map/ppermute | solution.py:577
  15.8 2.7 %collective-permute-done.2.y_ref = bf16[432,128]{1,0:T(8,128)(2,1)S(1)} collective-permute-done((bf16[432,128]{1,0:T(8,128)(2,1)S(1)}, bf16[432,128]{1,0:T(8,128)(2,1)S(1)}, u32[]{:S(2)}, u32[]{:S(2)}) %collective-permute-start.2) | collective-permute-done | bytes 110624 | tf_op jit(solution)/shard_map/ppermute | solution.py:577
  18.4 0.0 collective-permute-done.1.t_ref
  18.5 8.3 %collective-permute-start.3 = (bf16[240,128]{1,0:T(8,128)(2,1)S(1)}, bf16[240,128]{1,0:T(8,128)(2,1)S(1)}, u32[]{:S(2)}, u32[]{:S(2)}) collective-permute-start(bf16[240,128]{1,0:T(8,128)(2,1)S(1)} %pad_maximum_fusion.1), channel_id=1, source_target_pairs={{2,0},{4,2},{6,4},{8,6},{10,8},{12,10},{14,12},{0,14},{3,1},{5,3},... | collective-permute-start | bytes 184328 | tf_op jit(solution)/shard_map/ppermute | solution.py:577
  26.8 0.4 %hop_xy.1 = f32[288,128]{1,0:T(8,128)S(1)} custom-call(f32[384,128]{1,0:T(8,128)S(1)} %get-tuple-element.13.xs, f32[384,128]{1,0:T(8,128)S(1)} %get-tuple-element.14.ys, f32[16,128]{1,0:T(8,128)S(1)} %get-tuple-element.17.weights, bf16[432,128]{1,0:T(8,128)(2,1)S(1)} %collective-permute-done.2.y_ref), custom_call_target="tpu_custom_call" | custom-call | flops 2000000 | bytes 1000000 | tf_op jit(solution)/shard_map/hop_xy/pallas_call | solution.py:603
  27.2 0.5 %force_t.1 = (f32[144,128]{1,0:T(8,128)S(1)}, f32[144,128]{1,0:T(8,128)S(1)}) custom-call(f32[384,128]{1,0:T(8,128)S(1)} %get-tuple-element.13.xs, f32[384,128]{1,0:T(8,128)S(1)} %get-tuple-element.14.ys, f32[288,128]{1,0:T(8,128)S(1)} %get-tuple-element.15.us, f32[216,128]{1,0:T(8,128)S(1)} %get-tuple-element.16.ld, ...), custom_call_target="tpu_custom_call" | custom-call | flops 2000000 | bytes 1000000 | tf_op jit(solution)/shard_map/force_t/pallas_call | solution.py:606
  27.7 0.9 %collective-permute-done.3.z_ref = bf16[240,128]{1,0:T(8,128)(2,1)S(1)} collective-permute-done((bf16[240,128]{1,0:T(8,128)(2,1)S(1)}, bf16[240,128]{1,0:T(8,128)(2,1)S(1)}, u32[]{:S(2)}, u32[]{:S(2)}) %collective-permute-start.3) | collective-permute-done | bytes 61472 | tf_op jit(solution)/shard_map/ppermute | solution.py:577
  28.6 1.6 %force.1 = f32[288,128]{1,0:T(8,128)} custom-call(f32[384,128]{1,0:T(8,128)S(1)} %get-tuple-element.13.xs, f32[384,128]{1,0:T(8,128)S(1)} %get-tuple-element.14.ys, f32[288,128]{1,0:T(8,128)S(1)} %get-tuple-element.15.us, f32[216,128]{1,0:T(8,128)S(1)} %get-tuple-element.16.ld, f32[16,128]{1,0:T(8,128)S(1)} %get-tuple-element.17.weights, ...), custom_call_target="tpu_custom_call" | custom-call | flops 4000000 | bytes 1000000 | tf_op jit(solution)/shard_map/force/pallas_call | solution.py:614
  (7 shorter events, 0.1 us)
Async XLA Ops:
  1.2 10.2 %collective-permute-start = (bf16[144,128]{1,0:T(8,128)(2,1)S(1)}, bf16[144,128]{1,0:T(8,128)(2,1)S(1)}, u32[]{:S(2)}, u32[]{:S(2)}) collective-permute-start(bf16[144,128]{1,0:T(8,128)(2,1)S(1)} %get-tuple-element.18), channel_id=1, source_target_pairs={{16,0},{32,16},{48,32},{64,48},{80,64},{96,80},{112,96},{128,112},... | collective-permute-start | bytes 110600 | tf_op jit(solution)/shard_map/ppermute | solution.py:577
  9.1 9.4 %collective-permute-start.1 = (bf16[608,128]{1,0:T(8,128)(2,1)S(1)}, bf16[608,128]{1,0:T(8,128)(2,1)S(1)}, u32[]{:S(2)}, u32[]{:S(2)}) collective-permute-start(bf16[608,128]{1,0:T(8,128)(2,1)S(1)} %pack_t.1), channel_id=1, source_target_pairs={{16,0},{32,16},{48,32},{64,48},{80,64},{96,80},{112,96},{128,112},... | collective-permute-start | bytes 466952 | tf_op jit(solution)/shard_map/ppermute | solution.py:577
  11.4 7.0 %collective-permute-start.2 = (bf16[432,128]{1,0:T(8,128)(2,1)S(1)}, bf16[432,128]{1,0:T(8,128)(2,1)S(1)}, u32[]{:S(2)}, u32[]{:S(2)}) collective-permute-start(bf16[432,128]{1,0:T(8,128)(2,1)S(1)} %pad_maximum_fusion), channel_id=1, source_target_pairs={{1,0},{0,1},{3,2},{2,3},{5,4},{4,5},{7,6},{6,7},{9,8},{8,9},{11,10... | collective-permute-start | bytes 331784 | tf_op jit(solution)/shard_map/ppermute | solution.py:577
  18.5 10.2 %collective-permute-start.3 = (bf16[240,128]{1,0:T(8,128)(2,1)S(1)}, bf16[240,128]{1,0:T(8,128)(2,1)S(1)}, u32[]{:S(2)}, u32[]{:S(2)}) collective-permute-start(bf16[240,128]{1,0:T(8,128)(2,1)S(1)} %pad_maximum_fusion.1), channel_id=1, source_target_pairs={{2,0},{4,2},{6,4},{8,6},{10,8},{12,10},{14,12},{0,14},{3,1},{5,3},... | collective-permute-start | bytes 184328 | tf_op jit(solution)/shard_map/ppermute | solution.py:577

commit v3 on v2

--- a/solution.py
+++ b/solution.py
@@ -12,6 +12,8 @@
 T_PAIR = ((0, 3), (1, 3))
 Z_PAIRS = [((0, 2), (1, 2)), ((0, 1), (2, 3))]
 OFF = [(0, 1), (0, 2), (1, 2)]
+
+U_ROWS, LD_ROWS = 320, 256
 
 L_XT, L_ZT, L_CORNER, L_ROWS = 48, 84, 128, 144
 T_LINK, T_ROWS = 384, 608
@@ -146,7 +148,7 @@
             value = a + b if up_sign * low_sign > 0 else a - b
             row = (plane * 9 + e) * 8
             ls[row : row + 8, :] = value if up_sign > 0 else -value
-    ld[...] = ls[pl.ds(0, 216, stride=2), :] + ls[pl.ds(1, 216, stride=2), :]
+    ld[0:216, :] = ls[pl.ds(0, 216, stride=2), :] + ls[pl.ds(1, 216, stride=2), :]
 
 
 def plane_rows(m, n):
@@ -172,7 +174,7 @@
         weights[8 * p : 8 * p + 8, :] = jnp.where(even, coef[p], coef[p + 2])
     insertions(xs, ys, weights, ls, ld)
     copies[3].wait()
-    us[...] = u_ref[...].astype(F32)
+    us[0:288, :] = u_ref[...].astype(F32)
     ds[...] = jnp.zeros((L_ROWS, LANES), F32)
     ds[0:36, :] = ld[plane_rows(1, 3), :]
     ds[L_XT : L_XT + 36, :] = ld[plane_rows(0, 3), :]
@@ -583,7 +585,7 @@
         first_kernel,
         "insertions",
         [pl.BlockSpec(memory_space=pltpu.HBM)] * 4,
-        [(384, F32), (384, F32), (288, F32), (216, F32), (16, F32), (L_ROWS, BF16)],
+        [(384, F32), (384, F32), (U_ROWS, F32), (LD_ROWS, F32), (16, F32), (L_ROWS, BF16)],
         [pltpu.VMEM((384, LANES), BF16)] * 2
         + [pltpu.VMEM((288, LANES), BF16), pltpu.SMEM((4,), F32), 432, L_ROWS, pltpu.SemaphoreType.DMA((4,))],
         1000000,
@@ -616,7 +618,7 @@
         "force",
         [IN_VMEM] * 12,
         [(288, F32)],
-        [L_ROWS, T_ROWS - T_LINK, Y_ROWS + 48, Z_ROWS + 32, 400, 384, 144, 2 * G_ROWS, 432, 576],
+        [L_ROWS, T_ROWS - T_LINK, Y_ROWS + 48, Z_ROWS + 32, 400, 384, 144, 2 * G_ROWS, 432, 592],
         4000000,
         out_specs=pl.BlockSpec(),
     )(xs, ys, us, local, weights, tl_came, t_came, y_came, z_came, hop_xy, hop_t, acc_t)

time: 30.5 us -> 30.5 us (level)
  no operation moved by 1% of the time
where the time goes in v3:
time: 30.5 us; the launch traced here: 30.2 us
  starting transfers between devices  22.6 us (74%)
  Pallas kernels  3.93 us (13%)
  waiting for transfers between devices  3.6 us (12%)
    ppermute x4, starting transfers between devices, passed_back(): return lax.ppermute(block, axes if len(axes) > 1 else axes[0], route)  22.6 us
    ppermute x4, waiting for transfers between devices, passed_back(): return lax.ppermute(block, axes if len(axes) > 1 else axes[0], route)  3.6 us
    pallas_call x1, Pallas kernels, shards(): call(last_kernel, 'force', [IN_VMEM] * 12, [(288, F32)], [L_ROWS, T_ROWS...  1.62 us
    pallas_call x1, Pallas kernels, shards(): call(first_kernel, 'insertions', [pl.BlockSpec(memory_space=pltpu.HBM)] *...  1.2 us
  transfers between devices with their start and end apart: 4, of which 2 were waited for; matrix products, arithmetic and copies ran while one was open for 0% of the time, Pallas kernels for 4%

profile of v3, /device:TPU:2, one launch (start us, length us, event | category | flops | bytes accessed | tf_op | source)
XLA Modules:
  0.0 30.2 jit_solution(9508825932359452839)
XLA Ops:
  0.0 1.2 %insertions.1 = (f32[384,128]{1,0:T(8,128)S(1)}, f32[384,128]{1,0:T(8,128)S(1)}, f32[320,128]{1,0:T(8,128)S(1)}, f32[256,128]{1,0:T(8,128)S(1)}, f32[16,128]{1,0:T(8,128)S(1)}, /*index=5*/bf16[144,128]{1,0:T(8,128)(2,1)S(1)}) custom-call(bf16[384,128]{1,0:T(8,128)(2,1)} %bitcast.6, bf16[384,128]{1,0:T(8,128)(2,1)} %bitcast.7, bf16[288,128]{1,0:T(8,128)(2,1)} %bitcast.8, ...), custom_call_target="tpu_custom_call" | custom-call | flops 1000000 | bytes 1000000 | tf_op jit(solution)/shard_map/insertions/pallas_call | solution.py:584
  1.2 7.8 %collective-permute-start = (bf16[144,128]{1,0:T(8,128)(2,1)S(1)}, bf16[144,128]{1,0:T(8,128)(2,1)S(1)}, u32[]{:S(2)}, u32[]{:S(2)}) collective-permute-start(bf16[144,128]{1,0:T(8,128)(2,1)S(1)} %get-tuple-element.18), channel_id=1, source_target_pairs={{16,0},{32,16},{48,32},{64,48},{80,64},{96,80},{112,96},{128,112},... | collective-permute-start | bytes 110600 | tf_op jit(solution)/shard_map/ppermute | solution.py:579
  9.1 2.2 %collective-permute-start.1 = (bf16[608,128]{1,0:T(8,128)(2,1)S(1)}, bf16[608,128]{1,0:T(8,128)(2,1)S(1)}, u32[]{:S(2)}, u32[]{:S(2)}) collective-permute-start(bf16[608,128]{1,0:T(8,128)(2,1)S(1)} %pack_t.1), channel_id=1, source_target_pairs={{16,0},{32,16},{48,32},{64,48},{80,64},{96,80},{112,96},{128,112},... | collective-permute-start | bytes 466952 | tf_op jit(solution)/shard_map/ppermute | solution.py:579
  11.3 0.1 pack_y.1
  11.4 0.0 collective-permute-done.tl_ref
  11.4 4.3 %collective-permute-start.2 = (bf16[432,128]{1,0:T(8,128)(2,1)S(1)}, bf16[432,128]{1,0:T(8,128)(2,1)S(1)}, u32[]{:S(2)}, u32[]{:S(2)}) collective-permute-start(bf16[432,128]{1,0:T(8,128)(2,1)S(1)} %pad_maximum_fusion), channel_id=1, source_target_pairs={{1,0},{0,1},{3,2},{2,3},{5,4},{4,5},{7,6},{6,7},{9,8},{8,9},{11,10... | collective-permute-start | bytes 331784 | tf_op jit(solution)/shard_map/ppermute | solution.py:579
  15.8 2.7 %collective-permute-done.2.y_ref = bf16[432,128]{1,0:T(8,128)(2,1)S(1)} collective-permute-done((bf16[432,128]{1,0:T(8,128)(2,1)S(1)}, bf16[432,128]{1,0:T(8,128)(2,1)S(1)}, u32[]{:S(2)}, u32[]{:S(2)}) %collective-permute-start.2) | collective-permute-done | bytes 110624 | tf_op jit(solution)/shard_map/ppermute | solution.py:579
  18.4 0.0 collective-permute-done.1.t_ref
  18.5 8.3 %collective-permute-start.3 = (bf16[240,128]{1,0:T(8,128)(2,1)S(1)}, bf16[240,128]{1,0:T(8,128)(2,1)S(1)}, u32[]{:S(2)}, u32[]{:S(2)}) collective-permute-start(bf16[240,128]{1,0:T(8,128)(2,1)S(1)} %pad_maximum_fusion.1), channel_id=1, source_target_pairs={{2,0},{4,2},{6,4},{8,6},{10,8},{12,10},{14,12},{0,14},{3,1},{5,3},... | collective-permute-start | bytes 184328 | tf_op jit(solution)/shard_map/ppermute | solution.py:579
  26.8 0.4 %hop_xy.1 = f32[288,128]{1,0:T(8,128)S(1)} custom-call(f32[384,128]{1,0:T(8,128)S(1)} %get-tuple-element.13.xs, f32[384,128]{1,0:T(8,128)S(1)} %get-tuple-element.14.ys, f32[16,128]{1,0:T(8,128)S(1)} %get-tuple-element.17.weights, bf16[432,128]{1,0:T(8,128)(2,1)S(1)} %collective-permute-done.2.y_ref), custom_call_target="tpu_custom_call" | custom-call | flops 2000000 | bytes 1000000 | tf_op jit(solution)/shard_map/hop_xy/pallas_call | solution.py:605
  27.2 0.5 %force_t.1 = (f32[144,128]{1,0:T(8,128)S(1)}, f32[144,128]{1,0:T(8,128)S(1)}) custom-call(f32[384,128]{1,0:T(8,128)S(1)} %get-tuple-element.13.xs, f32[384,128]{1,0:T(8,128)S(1)} %get-tuple-element.14.ys, f32[320,128]{1,0:T(8,128)S(1)} %get-tuple-element.15.us, f32[256,128]{1,0:T(8,128)S(1)} %get-tuple-element.16.ld, ...), custom_call_target="tpu_custom_call" | custom-call | flops 2000000 | bytes 1000000 | tf_op jit(solution)/shard_map/force_t/pallas_call | solution.py:608
  27.7 0.9 %collective-permute-done.3.z_ref = bf16[240,128]{1,0:T(8,128)(2,1)S(1)} collective-permute-done((bf16[240,128]{1,0:T(8,128)(2,1)S(1)}, bf16[240,128]{1,0:T(8,128)(2,1)S(1)}, u32[]{:S(2)}, u32[]{:S(2)}) %collective-permute-start.3) | collective-permute-done | bytes 61472 | tf_op jit(solution)/shard_map/ppermute | solution.py:579
  28.6 1.6 %force.1 = f32[288,128]{1,0:T(8,128)} custom-call(f32[384,128]{1,0:T(8,128)S(1)} %get-tuple-element.13.xs, f32[384,128]{1,0:T(8,128)S(1)} %get-tuple-element.14.ys, f32[320,128]{1,0:T(8,128)S(1)} %get-tuple-element.15.us, f32[256,128]{1,0:T(8,128)S(1)} %get-tuple-element.16.ld, f32[16,128]{1,0:T(8,128)S(1)} %get-tuple-element.17.weights, ...), custom_call_target="tpu_custom_call" | custom-call | flops 4000000 | bytes 1000000 | tf_op jit(solution)/shard_map/force/pallas_call | solution.py:616
  (7 shorter events, 0.1 us)
Async XLA Ops:
  1.2 10.2 %collective-permute-start = (bf16[144,128]{1,0:T(8,128)(2,1)S(1)}, bf16[144,128]{1,0:T(8,128)(2,1)S(1)}, u32[]{:S(2)}, u32[]{:S(2)}) collective-permute-start(bf16[144,128]{1,0:T(8,128)(2,1)S(1)} %get-tuple-element.18), channel_id=1, source_target_pairs={{16,0},{32,16},{48,32},{64,48},{80,64},{96,80},{112,96},{128,112},... | collective-permute-start | bytes 110600 | tf_op jit(solution)/shard_map/ppermute | solution.py:579
  9.1 9.4 %collective-permute-start.1 = (bf16[608,128]{1,0:T(8,128)(2,1)S(1)}, bf16[608,128]{1,0:T(8,128)(2,1)S(1)}, u32[]{:S(2)}, u32[]{:S(2)}) collective-permute-start(bf16[608,128]{1,0:T(8,128)(2,1)S(1)} %pack_t.1), channel_id=1, source_target_pairs={{16,0},{32,16},{48,32},{64,48},{80,64},{96,80},{112,96},{128,112},... | collective-permute-start | bytes 466952 | tf_op jit(solution)/shard_map/ppermute | solution.py:579
  11.4 7.0 %collective-permute-start.2 = (bf16[432,128]{1,0:T(8,128)(2,1)S(1)}, bf16[432,128]{1,0:T(8,128)(2,1)S(1)}, u32[]{:S(2)}, u32[]{:S(2)}) collective-permute-start(bf16[432,128]{1,0:T(8,128)(2,1)S(1)} %pad_maximum_fusion), channel_id=1, source_target_pairs={{1,0},{0,1},{3,2},{2,3},{5,4},{4,5},{7,6},{6,7},{9,8},{8,9},{11,10... | collective-permute-start | bytes 331784 | tf_op jit(solution)/shard_map/ppermute | solution.py:579
  18.5 10.2 %collective-permute-start.3 = (bf16[240,128]{1,0:T(8,128)(2,1)S(1)}, bf16[240,128]{1,0:T(8,128)(2,1)S(1)}, u32[]{:S(2)}, u32[]{:S(2)}) collective-permute-start(bf16[240,128]{1,0:T(8,128)(2,1)S(1)} %pad_maximum_fusion.1), channel_id=1, source_target_pairs={{2,0},{4,2},{6,4},{8,6},{10,8},{12,10},{14,12},{0,14},{3,1},{5,3},... | collective-permute-start | bytes 184328 | tf_op jit(solution)/shard_map/ppermute | solution.py:579

commit v4 on v3

--- a/solution.py
+++ b/solution.py
@@ -18,7 +18,7 @@
 L_XT, L_ZT, L_CORNER, L_ROWS = 48, 84, 128, 144
 T_LINK, T_ROWS = 384, 608
 Y_REST, Y_HALF, Y_CORNER, Y_ROWS = 192, 168, 360, 384
-Z_LINK, Z_L, Z_ROWS = 96, 150, 192
+Z_LINK, Z_L, Z_CORNER, Z_ROWS = 96, 150, 177, 192
 
 G_UN1, G_UM1 = 8, 160
 G_LM, G_LN, G_LMN, G_L0 = 312, 392, 472, 552
@@ -216,7 +216,7 @@
         zs[Z_LINK + 18 * slot : Z_LINK + 18 * slot + 18, :] = us[pl.ds(72 * n, 18, stride=4), :]
         zs[Z_L + 9 * slot : Z_L + 9 * slot + 9, :] = ld[pl.ds(plane_rows(2, n).start, 9, stride=4), :]
     zs[Z_L + 27 : Z_ROWS, :] = jnp.zeros((Z_ROWS - Z_L - 27, LANES), F32)
-    zs[Z_ROWS : Z_ROWS + 16, :] = tl_ref[L_CORNER:L_ROWS, :].astype(F32)
+    zs[Z_CORNER : Z_CORNER + 9, :] = tl_ref[L_CORNER:L_ROWS, :].astype(F32)[0:9, :]
     z_out[...] = zs[...].astype(BF16)
 
 
@@ -402,12 +402,12 @@
             self.put(base, h, x_next(self.from_t(0)))
         elif m == 1 and n == 2:
             face = self.z_face(1)
-            came = self.zf[Z_ROWS + 16 : Z_ROWS + 25, :]
+            came = self.zf[Z_ROWS : Z_ROWS + 9, :]
             self.put_z(base, h, self.from_y(2), jnp.where(low_half(face), roll64(face), came))
         elif m == 1:
             self.put(base, h, self.y_next(self.from_t(1), roll64(self.yf[Y_ROWS : Y_ROWS + 36, :])))
         else:
-            self.put_z(base, h, self.from_t(2), self.zf[Z_ROWS : Z_ROWS + 9, :])
+            self.put_z(base, h, self.from_t(2), self.zf[Z_CORNER : Z_CORNER + 9, :])
 
     def stage(self, base, pair):
         for h in range(2):
@@ -484,7 +484,7 @@
     tl[...] = tl_ref[...].astype(F32)
     tf[...] = t_ref[T_LINK:T_ROWS, :].astype(F32)
     yf[...] = y_ref[...].astype(F32)
-    zf[...] = z_ref[0 : Z_ROWS + 32, :].astype(F32)
+    zf[...] = z_ref[0 : Z_ROWS + 16, :].astype(F32)
     for index, value in far_halves(xs, ys, 2):
         far[8 + 8 * index - 2 : 8 + 8 * index + 6, :] = value
     far[pl.ds(8 + 6, 48, stride=8), :] = zf[0:48, :]
@@ -595,7 +595,7 @@
     t_came = passed_back(to_t, "ta")
     (to_y,) = call(y_pack_kernel, "pack_y", [IN_VMEM] * 4, [(Y_ROWS, BF16)], [384, 336, Y_ROWS], 500000)(xs, ys, us, local)
     y_came = passed_back(jnp.concatenate([to_y, tl_came[0:48]]), "gy")
-    (to_z,) = call(z_pack_kernel, "pack_z", [IN_VMEM] * 5, [(Z_ROWS + 16, BF16)], [384, Z_ROWS + 16], 500000)(
+    (to_z,) = call(z_pack_kernel, "pack_z", [IN_VMEM] * 5, [(Z_ROWS, BF16)], [384, Z_ROWS], 500000)(
         xs, ys, us, local, tl_came
     )
     z_block = jnp.concatenate(
@@ -618,7 +618,7 @@
         "force",
         [IN_VMEM] * 12,
         [(288, F32)],
-        [L_ROWS, T_ROWS - T_LINK, Y_ROWS + 48, Z_ROWS + 32, 400, 384, 144, 2 * G_ROWS, 432, 592],
+        [L_ROWS, T_ROWS - T_LINK, Y_ROWS + 48, Z_ROWS + 16, 400, 384, 144, 2 * G_ROWS, 432, 592],
         4000000,
         out_specs=pl.BlockSpec(),
     )(xs, ys, us, local, weights, tl_came, t_came, y_came, z_came, hop_xy, hop_t, acc_t)

time: 30.5 us -> 30.4 us (level)
  no operation moved by 1% of the time
where the time goes in v4:
time: 30.4 us; the launch traced here: 30.2 us
  starting transfers between devices  22.6 us (74%)
  Pallas kernels  3.93 us (13%)
  waiting for transfers between devices  3.56 us (12%)
    ppermute x4, starting transfers between devices, passed_back(): return lax.ppermute(block, axes if len(axes) > 1 else axes[0], route)  22.6 us
    ppermute x4, waiting for transfers between devices, passed_back(): return lax.ppermute(block, axes if len(axes) > 1 else axes[0], route)  3.56 us
    pallas_call x1, Pallas kernels, shards(): call(last_kernel, 'force', [IN_VMEM] * 12, [(288, F32)], [L_ROWS, T_ROWS...  1.63 us
    pallas_call x1, Pallas kernels, shards(): call(first_kernel, 'insertions', [pl.BlockSpec(memory_space=pltpu.HBM)] *...  1.2 us
  transfers between devices with their start and end apart: 4, of which 2 were waited for; matrix products, arithmetic and copies ran while one was open for 0% of the time, Pallas kernels for 4%

profile of v4, /device:TPU:2, one launch (start us, length us, event | category | flops | bytes accessed | tf_op | source)
XLA Modules:
  0.0 30.2 jit_solution(8371911020224714449)
XLA Ops:
  0.0 1.2 %insertions.1 = (f32[384,128]{1,0:T(8,128)S(1)}, f32[384,128]{1,0:T(8,128)S(1)}, f32[320,128]{1,0:T(8,128)S(1)}, f32[256,128]{1,0:T(8,128)S(1)}, f32[16,128]{1,0:T(8,128)S(1)}, /*index=5*/bf16[144,128]{1,0:T(8,128)(2,1)S(1)}) custom-call(bf16[384,128]{1,0:T(8,128)(2,1)} %bitcast.6, bf16[384,128]{1,0:T(8,128)(2,1)} %bitcast.7, bf16[288,128]{1,0:T(8,128)(2,1)} %bitcast.8, ...), custom_call_target="tpu_custom_call" | custom-call | flops 1000000 | bytes 1000000 | tf_op jit(solution)/shard_map/insertions/pallas_call | solution.py:584
  1.2 7.8 %collective-permute-start = (bf16[144,128]{1,0:T(8,128)(2,1)S(1)}, bf16[144,128]{1,0:T(8,128)(2,1)S(1)}, u32[]{:S(2)}, u32[]{:S(2)}) collective-permute-start(bf16[144,128]{1,0:T(8,128)(2,1)S(1)} %get-tuple-element.18), channel_id=1, source_target_pairs={{16,0},{32,16},{48,32},{64,48},{80,64},{96,80},{112,96},{128,112},... | collective-permute-start | bytes 110600 | tf_op jit(solution)/shard_map/ppermute | solution.py:579
  9.1 2.2 %collective-permute-start.1 = (bf16[608,128]{1,0:T(8,128)(2,1)S(1)}, bf16[608,128]{1,0:T(8,128)(2,1)S(1)}, u32[]{:S(2)}, u32[]{:S(2)}) collective-permute-start(bf16[608,128]{1,0:T(8,128)(2,1)S(1)} %pack_t.1), channel_id=1, source_target_pairs={{16,0},{32,16},{48,32},{64,48},{80,64},{96,80},{112,96},{128,112},... | collective-permute-start | bytes 466952 | tf_op jit(solution)/shard_map/ppermute | solution.py:579
  11.3 0.1 pack_y.1
  11.4 0.0 collective-permute-done.tl_ref
  11.4 4.3 %collective-permute-start.2 = (bf16[432,128]{1,0:T(8,128)(2,1)S(1)}, bf16[432,128]{1,0:T(8,128)(2,1)S(1)}, u32[]{:S(2)}, u32[]{:S(2)}) collective-permute-start(bf16[432,128]{1,0:T(8,128)(2,1)S(1)} %pad_maximum_fusion), channel_id=1, source_target_pairs={{1,0},{0,1},{3,2},{2,3},{5,4},{4,5},{7,6},{6,7},{9,8},{8,9},{11,10... | collective-permute-start | bytes 331784 | tf_op jit(solution)/shard_map/ppermute | solution.py:579
  15.8 2.7 %collective-permute-done.2.y_ref = bf16[432,128]{1,0:T(8,128)(2,1)S(1)} collective-permute-done((bf16[432,128]{1,0:T(8,128)(2,1)S(1)}, bf16[432,128]{1,0:T(8,128)(2,1)S(1)}, u32[]{:S(2)}, u32[]{:S(2)}) %collective-permute-start.2) | collective-permute-done | bytes 110624 | tf_op jit(solution)/shard_map/ppermute | solution.py:579
  18.4 0.0 collective-permute-done.1.t_ref
  18.5 8.3 %collective-permute-start.3 = (bf16[224,128]{1,0:T(8,128)(2,1)S(1)}, bf16[224,128]{1,0:T(8,128)(2,1)S(1)}, u32[]{:S(2)}, u32[]{:S(2)}) collective-permute-start(bf16[224,128]{1,0:T(8,128)(2,1)S(1)} %pad_maximum_fusion.1), channel_id=1, source_target_pairs={{2,0},{4,2},{6,4},{8,6},{10,8},{12,10},{14,12},{0,14},{3,1},{5,3},... | collective-permute-start | bytes 172040 | tf_op jit(solution)/shard_map/ppermute | solution.py:579
  26.8 0.4 %hop_xy.1 = f32[288,128]{1,0:T(8,128)S(1)} custom-call(f32[384,128]{1,0:T(8,128)S(1)} %get-tuple-element.13.xs, f32[384,128]{1,0:T(8,128)S(1)} %get-tuple-element.14.ys, f32[16,128]{1,0:T(8,128)S(1)} %get-tuple-element.17.weights, bf16[432,128]{1,0:T(8,128)(2,1)S(1)} %collective-permute-done.2.y_ref), custom_call_target="tpu_custom_call" | custom-call | flops 2000000 | bytes 1000000 | tf_op jit(solution)/shard_map/hop_xy/pallas_call | solution.py:605
  27.2 0.5 %force_t.1 = (f32[144,128]{1,0:T(8,128)S(1)}, f32[144,128]{1,0:T(8,128)S(1)}) custom-call(f32[384,128]{1,0:T(8,128)S(1)} %get-tuple-element.13.xs, f32[384,128]{1,0:T(8,128)S(1)} %get-tuple-element.14.ys, f32[320,128]{1,0:T(8,128)S(1)} %get-tuple-element.15.us, f32[256,128]{1,0:T(8,128)S(1)} %get-tuple-element.16.ld, ...), custom_call_target="tpu_custom_call" | custom-call | flops 2000000 | bytes 1000000 | tf_op jit(solution)/shard_map/force_t/pallas_call | solution.py:608
  27.7 0.9 %collective-permute-done.3.z_ref = bf16[224,128]{1,0:T(8,128)(2,1)S(1)} collective-permute-done((bf16[224,128]{1,0:T(8,128)(2,1)S(1)}, bf16[224,128]{1,0:T(8,128)(2,1)S(1)}, u32[]{:S(2)}, u32[]{:S(2)}) %collective-permute-start.3) | collective-permute-done | bytes 57376 | tf_op jit(solution)/shard_map/ppermute | solution.py:579
  28.6 1.6 %force.1 = f32[288,128]{1,0:T(8,128)} custom-call(f32[384,128]{1,0:T(8,128)S(1)} %get-tuple-element.13.xs, f32[384,128]{1,0:T(8,128)S(1)} %get-tuple-element.14.ys, f32[320,128]{1,0:T(8,128)S(1)} %get-tuple-element.15.us, f32[256,128]{1,0:T(8,128)S(1)} %get-tuple-element.16.ld, f32[16,128]{1,0:T(8,128)S(1)} %get-tuple-element.17.weights, ...), custom_call_target="tpu_custom_call" | custom-call | flops 4000000 | bytes 1000000 | tf_op jit(solution)/shard_map/force/pallas_call | solution.py:616
  (7 shorter events, 0.1 us)
Async XLA Ops:
  1.2 10.2 %collective-permute-start = (bf16[144,128]{1,0:T(8,128)(2,1)S(1)}, bf16[144,128]{1,0:T(8,128)(2,1)S(1)}, u32[]{:S(2)}, u32[]{:S(2)}) collective-permute-start(bf16[144,128]{1,0:T(8,128)(2,1)S(1)} %get-tuple-element.18), channel_id=1, source_target_pairs={{16,0},{32,16},{48,32},{64,48},{80,64},{96,80},{112,96},{128,112},... | collective-permute-start | bytes 110600 | tf_op jit(solution)/shard_map/ppermute | solution.py:579
  9.1 9.4 %collective-permute-start.1 = (bf16[608,128]{1,0:T(8,128)(2,1)S(1)}, bf16[608,128]{1,0:T(8,128)(2,1)S(1)}, u32[]{:S(2)}, u32[]{:S(2)}) collective-permute-start(bf16[608,128]{1,0:T(8,128)(2,1)S(1)} %pack_t.1), channel_id=1, source_target_pairs={{16,0},{32,16},{48,32},{64,48},{80,64},{96,80},{112,96},{128,112},... | collective-permute-start | bytes 466952 | tf_op jit(solution)/shard_map/ppermute | solution.py:579
  11.4 7.0 %collective-permute-start.2 = (bf16[432,128]{1,0:T(8,128)(2,1)S(1)}, bf16[432,128]{1,0:T(8,128)(2,1)S(1)}, u32[]{:S(2)}, u32[]{:S(2)}) collective-permute-start(bf16[432,128]{1,0:T(8,128)(2,1)S(1)} %pad_maximum_fusion), channel_id=1, source_target_pairs={{1,0},{0,1},{3,2},{2,3},{5,4},{4,5},{7,6},{6,7},{9,8},{8,9},{11,10... | collective-permute-start | bytes 331784 | tf_op jit(solution)/shard_map/ppermute | solution.py:579
  18.5 10.1 %collective-permute-start.3 = (bf16[224,128]{1,0:T(8,128)(2,1)S(1)}, bf16[224,128]{1,0:T(8,128)(2,1)S(1)}, u32[]{:S(2)}, u32[]{:S(2)}) collective-permute-start(bf16[224,128]{1,0:T(8,128)(2,1)S(1)} %pad_maximum_fusion.1), channel_id=1, source_target_pairs={{2,0},{4,2},{6,4},{8,6},{10,8},{12,10},{14,12},{0,14},{3,1},{5,3},... | collective-permute-start | bytes 172040 | tf_op jit(solution)/shard_map/ppermute | solution.py:579

commit v5 on v4

--- a/solution.py
+++ b/solution.py
@@ -466,20 +466,21 @@
     lax.fori_loop(0, 2, one_hop, 0)
 
 
-def t_kernel(xs, ys, us, ld, weights, tl_ref, t_ref, y_ref, hop, acc, tl, tf, yf, near, geo, work):
+def t_kernel(xs, ys, us, ld, weights, tl_ref, t_ref, y_ref, hop, acc, near_z, tl, tf, yf, near, geo, work):
     tl[...] = tl_ref[...].astype(F32)
     tf[...] = t_ref[T_LINK:T_ROWS, :].astype(F32)
     yf[...] = y_ref[...].astype(F32)
     geo[920:1304, :] = t_ref[0:384, :].astype(F32)
     stage_near(xs, ys, weights, near, 0, 3)
+    stage_near(xs, ys, weights, near_z, 0, 2)
     hop_sums(geo, near, 920, 0, hop, 0)
     Neighbours(geo, us, ld, tf, tl, yf).stage(0, T_PAIR)
     plane_force(geo, 0, work, acc, 0)
 
 
 def last_kernel(
-    xs, ys, us, ld, weights, tl_ref, t_ref, y_ref, z_ref, hop_xy, hop_t, acc_t, out,
-    tl, tf, yf, zf, far, near, hop, geo, work, acc,
+    xs, ys, us, ld, tl_ref, t_ref, y_ref, z_ref, hop_xy, hop_t, acc_t, near, out,
+    tl, tf, yf, zf, far, hop, geo, work, acc,
 ):
     tl[...] = tl_ref[...].astype(F32)
     tf[...] = t_ref[T_LINK:T_ROWS, :].astype(F32)
@@ -489,7 +490,6 @@
         far[8 + 8 * index - 2 : 8 + 8 * index + 6, :] = value
     far[pl.ds(8 + 6, 48, stride=8), :] = zf[0:48, :]
     far[pl.ds(8 + 7, 48, stride=8), :] = zf[48:96, :]
-    stage_near(xs, ys, weights, near, 0, 2)
     hop_sums(far, near, 8, 0, hop, 0)
     places = Neighbours(geo, us, ld, tf, tl, yf, zf)
     for pair in range(2):
@@ -605,11 +605,11 @@
     (hop_xy,) = call(
         xy_kernel, "hop_xy", [IN_VMEM] * 4, [(288, F32)], [Y_REST, 768, 768], 2000000
     )(xs, ys, weights, y_came)
-    hop_t, acc_t = call(
+    hop_t, acc_t, near_z = call(
         t_kernel,
         "force_t",
         [IN_VMEM] * 8,
-        [(144, F32), (144, F32)],
+        [(144, F32), (144, F32), (384, F32)],
         [L_ROWS, T_ROWS - T_LINK, Y_ROWS + 48, 384, 1304, 432],
         2000000,
     )(xs, ys, us, local, weights, tl_came, t_came, y_came)
@@ -618,10 +618,10 @@
         "force",
         [IN_VMEM] * 12,
         [(288, F32)],
-        [L_ROWS, T_ROWS - T_LINK, Y_ROWS + 48, Z_ROWS + 16, 400, 384, 144, 2 * G_ROWS, 432, 592],
+        [L_ROWS, T_ROWS - T_LINK, Y_ROWS + 48, Z_ROWS + 16, 400, 144, 2 * G_ROWS, 432, 592],
         4000000,
         out_specs=pl.BlockSpec(),
-    )(xs, ys, us, local, weights, tl_came, t_came, y_came, z_came, hop_xy, hop_t, acc_t)
+    )(xs, ys, us, local, tl_came, t_came, y_came, z_came, hop_xy, hop_t, acc_t, near_z)
     return force.reshape(links.shape)
 
 

time: 30.4 us -> 30.4 us (level)
  no operation moved by 1% of the time
where the time goes in v5:
time: 30.4 us; the launch traced here: 30.2 us
  starting transfers between devices  22.6 us (74%)
  Pallas kernels  3.93 us (13%)
  waiting for transfers between devices  3.53 us (12%)
    ppermute x4, starting transfers between devices, passed_back(): return lax.ppermute(block, axes if len(axes) > 1 else axes[0], route)  22.6 us
    ppermute x4, waiting for transfers between devices, passed_back(): return lax.ppermute(block, axes if len(axes) > 1 else axes[0], route)  3.53 us
    pallas_call x1, Pallas kernels, shards(): call(last_kernel, 'force', [IN_VMEM] * 12, [(288, F32)], [L_ROWS, T_ROWS...  1.61 us
    pallas_call x1, Pallas kernels, shards(): call(first_kernel, 'insertions', [pl.BlockSpec(memory_space=pltpu.HBM)] *...  1.2 us
  transfers between devices with their start and end apart: 4, of which 2 were waited for; matrix products, arithmetic and copies ran while one was open for 0% of the time, Pallas kernels for 4%

profile of v5, /device:TPU:2, one launch (start us, length us, event | category | flops | bytes accessed | tf_op | source)
XLA Modules:
  0.0 30.2 jit_solution(14249290871209128274)
XLA Ops:
  0.0 1.2 %insertions.1 = (f32[384,128]{1,0:T(8,128)S(1)}, f32[384,128]{1,0:T(8,128)S(1)}, f32[320,128]{1,0:T(8,128)S(1)}, f32[256,128]{1,0:T(8,128)S(1)}, f32[16,128]{1,0:T(8,128)S(1)}, /*index=5*/bf16[144,128]{1,0:T(8,128)(2,1)S(1)}) custom-call(bf16[384,128]{1,0:T(8,128)(2,1)} %bitcast.6, bf16[384,128]{1,0:T(8,128)(2,1)} %bitcast.7, bf16[288,128]{1,0:T(8,128)(2,1)} %bitcast.8, ...), custom_call_target="tpu_custom_call" | custom-call | flops 1000000 | bytes 1000000 | tf_op jit(solution)/shard_map/insertions/pallas_call | solution.py:584
  1.2 7.8 %collective-permute-start = (bf16[144,128]{1,0:T(8,128)(2,1)S(1)}, bf16[144,128]{1,0:T(8,128)(2,1)S(1)}, u32[]{:S(2)}, u32[]{:S(2)}) collective-permute-start(bf16[144,128]{1,0:T(8,128)(2,1)S(1)} %get-tuple-element.18), channel_id=1, source_target_pairs={{16,0},{32,16},{48,32},{64,48},{80,64},{96,80},{112,96},{128,112},... | collective-permute-start | bytes 110600 | tf_op jit(solution)/shard_map/ppermute | solution.py:579
  9.1 2.2 %collective-permute-start.1 = (bf16[608,128]{1,0:T(8,128)(2,1)S(1)}, bf16[608,128]{1,0:T(8,128)(2,1)S(1)}, u32[]{:S(2)}, u32[]{:S(2)}) collective-permute-start(bf16[608,128]{1,0:T(8,128)(2,1)S(1)} %pack_t.1), channel_id=1, source_target_pairs={{16,0},{32,16},{48,32},{64,48},{80,64},{96,80},{112,96},{128,112},... | collective-permute-start | bytes 466952 | tf_op jit(solution)/shard_map/ppermute | solution.py:579
  11.3 0.1 pack_y.1
  11.4 0.0 collective-permute-done.tl_ref
  11.4 4.3 %collective-permute-start.2 = (bf16[432,128]{1,0:T(8,128)(2,1)S(1)}, bf16[432,128]{1,0:T(8,128)(2,1)S(1)}, u32[]{:S(2)}, u32[]{:S(2)}) collective-permute-start(bf16[432,128]{1,0:T(8,128)(2,1)S(1)} %pad_maximum_fusion), channel_id=1, source_target_pairs={{1,0},{0,1},{3,2},{2,3},{5,4},{4,5},{7,6},{6,7},{9,8},{8,9},{11,10... | collective-permute-start | bytes 331784 | tf_op jit(solution)/shard_map/ppermute | solution.py:579
  15.8 2.7 %collective-permute-done.2.y_ref = bf16[432,128]{1,0:T(8,128)(2,1)S(1)} collective-permute-done((bf16[432,128]{1,0:T(8,128)(2,1)S(1)}, bf16[432,128]{1,0:T(8,128)(2,1)S(1)}, u32[]{:S(2)}, u32[]{:S(2)}) %collective-permute-start.2) | collective-permute-done | bytes 110624 | tf_op jit(solution)/shard_map/ppermute | solution.py:579
  18.4 0.0 collective-permute-done.1.t_ref
  18.5 8.3 %collective-permute-start.3 = (bf16[224,128]{1,0:T(8,128)(2,1)S(1)}, bf16[224,128]{1,0:T(8,128)(2,1)S(1)}, u32[]{:S(2)}, u32[]{:S(2)}) collective-permute-start(bf16[224,128]{1,0:T(8,128)(2,1)S(1)} %pad_maximum_fusion.1), channel_id=1, source_target_pairs={{2,0},{4,2},{6,4},{8,6},{10,8},{12,10},{14,12},{0,14},{3,1},{5,3},... | collective-permute-start | bytes 172040 | tf_op jit(solution)/shard_map/ppermute | solution.py:579
  26.8 0.4 %hop_xy.1 = f32[288,128]{1,0:T(8,128)S(1)} custom-call(f32[384,128]{1,0:T(8,128)S(1)} %get-tuple-element.14.xs, f32[384,128]{1,0:T(8,128)S(1)} %get-tuple-element.15.ys, f32[16,128]{1,0:T(8,128)S(1)} %get-tuple-element.19.weights, bf16[432,128]{1,0:T(8,128)(2,1)S(1)} %collective-permute-done.2.y_ref), custom_call_target="tpu_custom_call" | custom-call | flops 2000000 | bytes 1000000 | tf_op jit(solution)/shard_map/hop_xy/pallas_call | solution.py:605
  27.2 0.5 %force_t.1 = (f32[144,128]{1,0:T(8,128)S(1)}, f32[144,128]{1,0:T(8,128)S(1)}, f32[384,128]{1,0:T(8,128)S(1)}) custom-call(f32[384,128]{1,0:T(8,128)S(1)} %get-tuple-element.14.xs, f32[384,128]{1,0:T(8,128)S(1)} %get-tuple-element.15.ys, f32[320,128]{1,0:T(8,128)S(1)} %get-tuple-element.16.us, f32[256,128]{1,0:T(8,128)S(1)} %get-tuple-element.17.ld, ...), custom_call_target="tpu_custom_call" | custom-call | flops 2000000 | bytes 1000000 | tf_op jit(solution)/shard_map/force_t/pallas_call | solution.py:608
  27.7 0.9 %collective-permute-done.3.z_ref = bf16[224,128]{1,0:T(8,128)(2,1)S(1)} collective-permute-done((bf16[224,128]{1,0:T(8,128)(2,1)S(1)}, bf16[224,128]{1,0:T(8,128)(2,1)S(1)}, u32[]{:S(2)}, u32[]{:S(2)}) %collective-permute-start.3) | collective-permute-done | bytes 57376 | tf_op jit(solution)/shard_map/ppermute | solution.py:579
  28.6 1.6 %force.1 = f32[288,128]{1,0:T(8,128)} custom-call(f32[384,128]{1,0:T(8,128)S(1)} %get-tuple-element.14.xs, f32[384,128]{1,0:T(8,128)S(1)} %get-tuple-element.15.ys, f32[320,128]{1,0:T(8,128)S(1)} %get-tuple-element.16.us, f32[256,128]{1,0:T(8,128)S(1)} %get-tuple-element.17.ld, bf16[144,128]{1,0:T(8,128)(2,1)S(1)} %collective-permute-done.tl_ref, ...), custom_call_target="tpu_custom_call" | custom-call | flops 4000000 | bytes 1000000 | tf_op jit(solution)/shard_map/force/pallas_call | solution.py:616
  (7 shorter events, 0.1 us)
Async XLA Ops:
  1.2 10.2 %collective-permute-start = (bf16[144,128]{1,0:T(8,128)(2,1)S(1)}, bf16[144,128]{1,0:T(8,128)(2,1)S(1)}, u32[]{:S(2)}, u32[]{:S(2)}) collective-permute-start(bf16[144,128]{1,0:T(8,128)(2,1)S(1)} %get-tuple-element.18), channel_id=1, source_target_pairs={{16,0},{32,16},{48,32},{64,48},{80,64},{96,80},{112,96},{128,112},... | collective-permute-start | bytes 110600 | tf_op jit(solution)/shard_map/ppermute | solution.py:579
  9.1 9.4 %collective-permute-start.1 = (bf16[608,128]{1,0:T(8,128)(2,1)S(1)}, bf16[608,128]{1,0:T(8,128)(2,1)S(1)}, u32[]{:S(2)}, u32[]{:S(2)}) collective-permute-start(bf16[608,128]{1,0:T(8,128)(2,1)S(1)} %pack_t.1), channel_id=1, source_target_pairs={{16,0},{32,16},{48,32},{64,48},{80,64},{96,80},{112,96},{128,112},... | collective-permute-start | bytes 466952 | tf_op jit(solution)/shard_map/ppermute | solution.py:579
  11.4 7.0 %collective-permute-start.2 = (bf16[432,128]{1,0:T(8,128)(2,1)S(1)}, bf16[432,128]{1,0:T(8,128)(2,1)S(1)}, u32[]{:S(2)}, u32[]{:S(2)}) collective-permute-start(bf16[432,128]{1,0:T(8,128)(2,1)S(1)} %pad_maximum_fusion), channel_id=1, source_target_pairs={{1,0},{0,1},{3,2},{2,3},{5,4},{4,5},{7,6},{6,7},{9,8},{8,9},{11,10... | collective-permute-start | bytes 331784 | tf_op jit(solution)/shard_map/ppermute | solution.py:579
  18.5 10.1 %collective-permute-start.3 = (bf16[224,128]{1,0:T(8,128)(2,1)S(1)}, bf16[224,128]{1,0:T(8,128)(2,1)S(1)}, u32[]{:S(2)}, u32[]{:S(2)}) collective-permute-start(bf16[224,128]{1,0:T(8,128)(2,1)S(1)} %pad_maximum_fusion.1), channel_id=1, source_target_pairs={{2,0},{4,2},{6,4},{8,6},{10,8},{12,10},{14,12},{0,14},{3,1},{5,3},... | collective-permute-start | bytes 172040 | tf_op jit(solution)/shard_map/ppermute | solution.py:579
